TPU v7x, 512 devices: a whole 4x4x16 slice. The times are simulated.
512 devices in a mesh: gx: 32 (over z, core), gy: 8 (over y, x_lo), gz: 2 (over x_hi).
Axes of the slice: x: 4 (x_hi: 2, x_lo: 2; x = x_hi * 2 + x_lo), y: 4, z: 16, core: 2. Of those that a mesh axis runs over, the one named last changes fastest.
Arguments:
- adjoint: float32 [2, 4, 16, 256, 1024], P(None, None, 'gz', 'gx', 'gy'), may hold values from -6 to 6
- saved_state: float32 [4, 4, 16, 256, 1024], P(None, None, 'gz', 'gx', 'gy'), may hold values from -6 to 6
- wind_field: float32 [3, 16, 256, 1024], P(None, 'gz', 'gx', 'gy'), may hold values from -0.3 to 0.3
- facade_slot: int32 [16, 256, 1024], P('gz', 'gx', 'gy'), may hold values from 0 to 64, as said below
- facade_table: int32 [2, 32, 8, 64], P('gz', 'gx', 'gy'), may hold values from 0 to 16383, as said below
- impedance: float32 [16384], replicated, may hold values from 0.1 to 1
Outputs:
- adjoint_out: float32 [2, 4, 16, 256, 1024], P(None, None, 'gz', 'gx', 'gy')
- gradient: float32 [16384], P(('gx', 'gy', 'gz'))
Inputs may be any that keep to these rules, and one draw needn't show every extreme that they name: `facade_slot`: slots name entries of the cell's own device block table. `facade_table`: A block's facades are owned by that block's device or by one of the two devices beside it along gx (wrapping), the owner of facade f being the device of index f // 32 along gx+gy+gz; ids may repeat within and across tables.
All inputs are finite; a program needn't handle non-finite values.
Results may differ from a plain program's by a relative error of at most 0.00013.
Values sent between devices are 32-bit elements; how exact they have to be, the bound alone decides.
A program may use at most 64 MiB of HBM per device.

v0:
```python
import jax
import jax.numpy as jnp
from jax import lax
from jax.sharding import PartitionSpec as P

FAC_DEV = 32


TIME_STEP = 0.3


def padded(cells, sides, width):
    for axis, dim in sides:
        count = lax.axis_size(axis)
        ends = count - 1
        head = lax.slice_in_dim(cells, 0, width, axis=dim)
        tail = lax.slice_in_dim(cells, cells.shape[dim] - width, cells.shape[dim], axis=dim)
        cells = jnp.concatenate(
            [
                lax.ppermute(tail, axis, [(i, (i + 1) % count) for i in range(ends)]),
                cells,
                lax.ppermute(head, axis, [((i + 1) % count, i) for i in range(ends)]),
            ],
            axis=dim,
        )
    return cells


def shifted(block, axis, distance):
    devices = range(lax.axis_size(axis))
    route = [((i - distance) % len(devices), i) for i in devices]
    return lax.ppermute(block, axis, route)


def trimmed(field, axis_k, offset):
    selector = [slice(None)] * field.ndim
    for j in range(3):
        dim = field.ndim - 3 + j
        length = field.shape[dim]
        if j == axis_k:
            selector[dim] = slice(1 + offset, length - 1 + offset)
        else:
            selector[dim] = slice(1, length - 1)
    return field[tuple(selector)]


def interior(field):
    return trimmed(field, 0, 0)


def central_diff(field, axis_k):
    return 0.5 * (trimmed(field, axis_k, 1) - trimmed(field, axis_k, -1))


def tendency(state_pad, wind_pad, damping_pad):
    pressure = state_pad[0]
    damping = interior(damping_pad)
    result = []
    for index in range(4):
        component = state_pad[index]
        advection = (
            central_diff(wind_pad[0] * component, 0)
            + central_diff(wind_pad[1] * component, 1)
            + central_diff(wind_pad[2] * component, 2)
        )
        if index == 0:
            coupling = (
                central_diff(state_pad[1], 0)
                + central_diff(state_pad[2], 1)
                + central_diff(state_pad[3], 2)
            )
        else:
            coupling = central_diff(pressure, index - 1)
        result.append(advection + coupling - damping * interior(component))
    return jnp.stack(result)


def owner_bucket(slot_names, slot_terms, offset):
    index_x = lax.axis_index("gx")
    index_y = lax.axis_index("gy")
    index_z = lax.axis_index("gz")
    count_x = lax.axis_size("gx")
    count_y = lax.axis_size("gy")
    count_z = lax.axis_size("gz")
    owner = ((index_x + offset + count_x) % count_x * count_y + index_y) * count_z + index_z
    targets = owner * FAC_DEV + jnp.arange(FAC_DEV, dtype=jnp.int32)
    return jnp.sum(
        jnp.where(slot_names[:, None] == targets[None, :], slot_terms[:, None], jnp.float32(0.0)),
        axis=0,
    )


def local(adjoint, saved_state, wind_field, facade_slot, facade_table, impedance):
    depth_z, depth_x, depth_y = facade_slot.shape
    slot_names = facade_table.reshape(-1)
    slot_count = slot_names.shape[0]
    local_damping = impedance[slot_names]
    levels = jnp.arange(1, slot_count + 1, dtype=jnp.int32)
    one_hot = (facade_slot[None] == levels[:, None, None, None]).astype(jnp.float32)
    damping = jnp.tensordot(local_damping, one_hot, axes=1, precision=lax.Precision.HIGHEST)
    static = jnp.concatenate([wind_field, damping[None]], axis=0)
    width = 1
    static_pad = padded(static, (("gx", 2), ("gy", 3), ("gz", 1)), width)
    upper = adjoint[0]
    middle = adjoint[1]
    products = jnp.zeros((depth_z, depth_x, depth_y), jnp.float32)
    step_count = saved_state.shape[0]
    for step in range(step_count):
        products = products + jnp.sum(middle * saved_state[step], axis=0)
        middle_pad = padded(middle, (("gx", 2), ("gy", 3), ("gz", 1)), 1)
        newest = upper + 2.0 * TIME_STEP * tendency(middle_pad, static_pad[:3], static_pad[3])
        upper, middle = (middle, newest)
    terms = -2.0 * TIME_STEP * products
    slot_terms = jnp.tensordot(one_hot, terms, axes=3, precision=lax.Precision.HIGHEST)
    own_part = owner_bucket(slot_names, slot_terms, 0)
    upward = owner_bucket(slot_names, slot_terms, 1)
    downward = owner_bucket(slot_names, slot_terms, -1)
    lower_part = shifted(upward, "gx", 1)
    upper_part = shifted(downward, "gx", -1)
    gradient = own_part + lower_part + upper_part
    return (jnp.stack([upper, middle]), gradient)


def solution(mesh):
    return jax.shard_map(
        local,
        mesh=mesh,
        in_specs=(
            P(None, None, "gz", "gx", "gy"),
            P(None, None, "gz", "gx", "gy"),
            P(None, "gz", "gx", "gy"),
            P("gz", "gx", "gy"),
            P("gz", "gx", "gy", None),
            P(),
        ),
        out_specs=(P(None, None, "gz", "gx", "gy"), P(("gx", "gy", "gz"))),
        check_vma=False,
    )
```

profile of v0, /device:TPU:128, one launch (start us, length us, event | category | flops | bytes accessed | tf_op | source)
XLA Modules:
  0.0 164.9 jit_solution(3028715814775150080)
XLA Ops:
  1.4 1.1 broadcast_compare_fusion
  2.5 0.8 gather_fusion
  4.2 1.9 %collective-permute-start = (f32[4,8,1,128]{3,2,1,0:T(1,128)S(1)}, f32[4,8,1,128]{3,2,1,0:T(1,128)S(1)}, u32[]{:S(2)}, u32[]{:S(2)}) collective-permute-start(f32[4,8,1,128]{3,2,1,0:T(1,128)S(1)} %get-tuple-element.102), channel_id=1, source_target_pairs={{0,16},{16,32},{32,48},{48,64},{64,80},{80,96},{96,112},{112,128},... | collective-permute-start | bytes 49160 | tf_op jit(solution)/shard_map/ppermute | solution.py:20
  6.1 4.9 %collective-permute-start.1 = (f32[4,8,1,128]{3,2,1,0:T(1,128)S(1)}, f32[4,8,1,128]{3,2,1,0:T(1,128)S(1)}, u32[]{:S(2)}, u32[]{:S(2)}) collective-permute-start(f32[4,8,1,128]{3,2,1,0:T(1,128)S(1)} %get-tuple-element.103), channel_id=1, source_target_pairs={{16,0},{32,16},{48,32},{64,48},{80,64},{96,80},{112,96},{128,112},... | collective-permute-start | bytes 49160 | tf_op jit(solution)/shard_map/ppermute | solution.py:22
  11.0 1.9 %collective-permute-start.6 = (f32[4,8,1,128]{3,2,1,0:T(1,128)S(1)}, f32[4,8,1,128]{3,2,1,0:T(1,128)S(1)}, u32[]{:S(2)}, u32[]{:S(2)}) collective-permute-start(f32[4,8,1,128]{3,2,1,0:T(1,128)S(1)} %get-tuple-element.104), channel_id=1, source_target_pairs={{0,16},{16,32},{32,48},{48,64},{64,80},{80,96},{96,112},{112,128},... | collective-permute-start | bytes 49160 | tf_op jit(solution)/shard_map/ppermute | solution.py:20
  13.0 4.9 %collective-permute-start.7 = (f32[4,8,1,128]{3,2,1,0:T(1,128)S(1)}, f32[4,8,1,128]{3,2,1,0:T(1,128)S(1)}, u32[]{:S(2)}, u32[]{:S(2)}) collective-permute-start(f32[4,8,1,128]{3,2,1,0:T(1,128)S(1)} %get-tuple-element.105), channel_id=1, source_target_pairs={{16,0},{32,16},{48,32},{64,48},{80,64},{96,80},{112,96},{128,112},... | collective-permute-start | bytes 49160 | tf_op jit(solution)/shard_map/ppermute | solution.py:22
  18.0 3.4 %collective-permute-start.2 = (f32[4,8,10,1]{3,2,1,0:T(8,128)S(1)}, f32[4,8,10,1]{3,2,1,0:T(8,128)S(1)}, u32[]{:S(2)}, u32[]{:S(2)}) collective-permute-start(f32[4,8,10,1]{3,2,1,0:T(8,128)S(1)} %get-tuple-element.92), channel_id=1, source_target_pairs={{0,2},{2,4},{4,6},{6,8},{8,10},{10,12},{12,14},{1,3},{3,5},{5,7},{... | collective-permute-start | bytes 3848 | tf_op jit(solution)/shard_map/ppermute | solution.py:20
  21.5 1.3 collective-permute-start.3
  23.0 4.6 %collective-permute-start.8 = (f32[4,8,10,1]{3,2,1,0:T(8,128)S(1)}, f32[4,8,10,1]{3,2,1,0:T(8,128)S(1)}, u32[]{:S(2)}, u32[]{:S(2)}) collective-permute-start(f32[4,8,10,1]{3,2,1,0:T(8,128)S(1)} %get-tuple-element.94), channel_id=1, source_target_pairs={{0,2},{2,4},{4,6},{6,8},{8,10},{10,12},{12,14},{1,3},{3,5},{5,7},{... | collective-permute-start | bytes 3848 | tf_op jit(solution)/shard_map/ppermute | solution.py:20
  27.5 1.3 collective-permute-start.9
  28.8 7.0 %collective-permute-done.3 = f32[4,8,10,1]{3,2,1,0:T(8,128)S(1)} collective-permute-done((f32[4,8,10,1]{3,2,1,0:T(8,128)S(1)}, f32[4,8,10,1]{3,2,1,0:T(8,128)S(1)}, u32[]{:S(2)}, u32[]{:S(2)}) %collective-permute-start.3) | collective-permute-done | bytes 1312 | tf_op jit(solution)/shard_map/ppermute | solution.py:22
  36.0 4.9 %collective-permute-start.4 = (f32[4,1,10,130]{3,2,1,0:T(8,128)S(1)}, f32[4,1,10,130]{3,2,1,0:T(8,128)S(1)}, u32[]{:S(2)}, u32[]{:S(2)}) collective-permute-start(f32[4,1,10,130]{3,2,1,0:T(8,128)S(1)} %get-tuple-element.64), channel_id=1, source_target_pairs={{0,1},{2,3},{4,5},{6,7},{8,9},{10,11},{12,13},{14,15},{16,17},{18,... | collective-permute-start | bytes 62408 | tf_op jit(solution)/shard_map/ppermute | solution.py:20
  40.9 1.3 collective-permute-start.5
  42.2 2.4 %collective-permute-done.9 = f32[4,8,10,1]{3,2,1,0:T(8,128)S(1)} collective-permute-done((f32[4,8,10,1]{3,2,1,0:T(8,128)S(1)}, f32[4,8,10,1]{3,2,1,0:T(8,128)S(1)}, u32[]{:S(2)}, u32[]{:S(2)}) %collective-permute-start.9) | collective-permute-done | bytes 1312 | tf_op jit(solution)/shard_map/ppermute | solution.py:22
  44.7 4.9 %collective-permute-start.10 = (f32[4,1,10,130]{3,2,1,0:T(8,128)S(1)}, f32[4,1,10,130]{3,2,1,0:T(8,128)S(1)}, u32[]{:S(2)}, u32[]{:S(2)}) collective-permute-start(f32[4,1,10,130]{3,2,1,0:T(8,128)S(1)} %get-tuple-element.66), channel_id=1, source_target_pairs={{0,1},{2,3},{4,5},{6,7},{8,9},{10,11},{12,13},{14,15},{16,17},{18,... | collective-permute-start | bytes 62408 | tf_op jit(solution)/shard_map/ppermute | solution.py:20
  49.7 1.3 collective-permute-start.11
  51.6 5.8 %collective-permute-done.11 = f32[4,1,10,130]{3,2,1,0:T(8,128)S(1)} collective-permute-done((f32[4,1,10,130]{3,2,1,0:T(8,128)S(1)}, f32[4,1,10,130]{3,2,1,0:T(8,128)S(1)}, u32[]{:S(2)}, u32[]{:S(2)}) %collective-permute-start.11) | collective-permute-done | bytes 20832 | tf_op jit(solution)/shard_map/ppermute | solution.py:22
  58.8 1.9 %collective-permute-start.12 = (f32[4,8,1,128]{3,2,1,0:T(1,128)S(1)}, f32[4,8,1,128]{3,2,1,0:T(1,128)S(1)}, u32[]{:S(2)}, u32[]{:S(2)}) collective-permute-start(f32[4,8,1,128]{3,2,1,0:T(1,128)S(1)} %get-tuple-element.100), channel_id=1, source_target_pairs={{0,16},{16,32},{32,48},{48,64},{64,80},{80,96},{96,112},{112,128},... | collective-permute-start | bytes 49160 | tf_op jit(solution)/shard_map/ppermute | solution.py:20
  60.7 4.9 %collective-permute-start.13 = (f32[4,8,1,128]{3,2,1,0:T(1,128)S(1)}, f32[4,8,1,128]{3,2,1,0:T(1,128)S(1)}, u32[]{:S(2)}, u32[]{:S(2)}) collective-permute-start(f32[4,8,1,128]{3,2,1,0:T(1,128)S(1)} %get-tuple-element.101), channel_id=1, source_target_pairs={{16,0},{32,16},{48,32},{64,48},{80,64},{96,80},{112,96},{128,112},... | collective-permute-start | bytes 49160 | tf_op jit(solution)/shard_map/ppermute | solution.py:22
  65.6 1.4 collective-permute-done.13
  67.2 2.8 %collective-permute-start.14 = (f32[4,8,10,1]{3,2,1,0:T(8,128)S(1)}, f32[4,8,10,1]{3,2,1,0:T(8,128)S(1)}, u32[]{:S(2)}, u32[]{:S(2)}) collective-permute-start(f32[4,8,10,1]{3,2,1,0:T(8,128)S(1)} %get-tuple-element.90), channel_id=1, source_target_pairs={{0,2},{2,4},{4,6},{6,8},{8,10},{10,12},{12,14},{1,3},{3,5},{5,7},{... | collective-permute-start | bytes 3848 | tf_op jit(solution)/shard_map/ppermute | solution.py:20
  70.0 1.3 collective-permute-start.15
  71.3 4.8 %collective-permute-done.14 = f32[4,8,10,1]{3,2,1,0:T(8,128)S(1)} collective-permute-done((f32[4,8,10,1]{3,2,1,0:T(8,128)S(1)}, f32[4,8,10,1]{3,2,1,0:T(8,128)S(1)}, u32[]{:S(2)}, u32[]{:S(2)}) %collective-permute-start.14) | collective-permute-done | bytes 1312 | tf_op jit(solution)/shard_map/ppermute | solution.py:20
  76.1 8.5 %collective-permute-done.15 = f32[4,8,10,1]{3,2,1,0:T(8,128)S(1)} collective-permute-done((f32[4,8,10,1]{3,2,1,0:T(8,128)S(1)}, f32[4,8,10,1]{3,2,1,0:T(8,128)S(1)}, u32[]{:S(2)}, u32[]{:S(2)}) %collective-permute-start.15) | collective-permute-done | bytes 1312 | tf_op jit(solution)/shard_map/ppermute | solution.py:22
  84.8 1.6 collective-permute-start.16
  86.4 1.3 collective-permute-start.17
  88.3 5.8 %collective-permute-done.17 = f32[4,1,10,130]{3,2,1,0:T(8,128)S(1)} collective-permute-done((f32[4,1,10,130]{3,2,1,0:T(8,128)S(1)}, f32[4,1,10,130]{3,2,1,0:T(8,128)S(1)}, u32[]{:S(2)}, u32[]{:S(2)}) %collective-permute-start.17) | collective-permute-done | bytes 20832 | tf_op jit(solution)/shard_map/ppermute | solution.py:22
  95.5 1.9 %collective-permute-start.18 = (f32[4,8,1,128]{3,2,1,0:T(1,128)S(1)}, f32[4,8,1,128]{3,2,1,0:T(1,128)S(1)}, u32[]{:S(2)}, u32[]{:S(2)}) collective-permute-start(f32[4,8,1,128]{3,2,1,0:T(1,128)S(1)} %get-tuple-element.98), channel_id=1, source_target_pairs={{0,16},{16,32},{32,48},{48,64},{64,80},{80,96},{96,112},{112,128},... | collective-permute-start | bytes 49160 | tf_op jit(solution)/shard_map/ppermute | solution.py:20
  97.4 4.9 %collective-permute-start.19 = (f32[4,8,1,128]{3,2,1,0:T(1,128)S(1)}, f32[4,8,1,128]{3,2,1,0:T(1,128)S(1)}, u32[]{:S(2)}, u32[]{:S(2)}) collective-permute-start(f32[4,8,1,128]{3,2,1,0:T(1,128)S(1)} %get-tuple-element.99), channel_id=1, source_target_pairs={{16,0},{32,16},{48,32},{64,48},{80,64},{96,80},{112,96},{128,112},... | collective-permute-start | bytes 49160 | tf_op jit(solution)/shard_map/ppermute | solution.py:22
  102.3 1.4 collective-permute-done.19
  103.9 2.5 %collective-permute-start.20 = (f32[4,8,10,1]{3,2,1,0:T(8,128)S(1)}, f32[4,8,10,1]{3,2,1,0:T(8,128)S(1)}, u32[]{:S(2)}, u32[]{:S(2)}) collective-permute-start(f32[4,8,10,1]{3,2,1,0:T(8,128)S(1)} %get-tuple-element.88), channel_id=1, source_target_pairs={{0,2},{2,4},{4,6},{6,8},{8,10},{10,12},{12,14},{1,3},{3,5},{5,7},{... | collective-permute-start | bytes 3848 | tf_op jit(solution)/shard_map/ppermute | solution.py:20
  106.4 1.3 collective-permute-start.21
  107.7 3.4 %collective-permute-done.20 = f32[4,8,10,1]{3,2,1,0:T(8,128)S(1)} collective-permute-done((f32[4,8,10,1]{3,2,1,0:T(8,128)S(1)}, f32[4,8,10,1]{3,2,1,0:T(8,128)S(1)}, u32[]{:S(2)}, u32[]{:S(2)}) %collective-permute-start.20) | collective-permute-done | bytes 1312 | tf_op jit(solution)/shard_map/ppermute | solution.py:20
  111.1 8.2 %collective-permute-done.21 = f32[4,8,10,1]{3,2,1,0:T(8,128)S(1)} collective-permute-done((f32[4,8,10,1]{3,2,1,0:T(8,128)S(1)}, f32[4,8,10,1]{3,2,1,0:T(8,128)S(1)}, u32[]{:S(2)}, u32[]{:S(2)}) %collective-permute-start.21) | collective-permute-done | bytes 1312 | tf_op jit(solution)/shard_map/ppermute | solution.py:22
  119.5 1.5 collective-permute-start.22
  121.0 1.3 collective-permute-start.23
  122.8 5.8 %collective-permute-done.23 = f32[4,1,10,130]{3,2,1,0:T(8,128)S(1)} collective-permute-done((f32[4,1,10,130]{3,2,1,0:T(8,128)S(1)}, f32[4,1,10,130]{3,2,1,0:T(8,128)S(1)}, u32[]{:S(2)}, u32[]{:S(2)}) %collective-permute-start.23) | collective-permute-done | bytes 20832 | tf_op jit(solution)/shard_map/ppermute | solution.py:22
  130.7 1.9 %collective-permute-start.24 = (f32[4,8,1,128]{3,2,1,0:T(1,128)S(1)}, f32[4,8,1,128]{3,2,1,0:T(1,128)S(1)}, u32[]{:S(2)}, u32[]{:S(2)}) collective-permute-start(f32[4,8,1,128]{3,2,1,0:T(1,128)S(1)} %get-tuple-element.96), channel_id=1, source_target_pairs={{0,16},{16,32},{32,48},{48,64},{64,80},{80,96},{96,112},{112,128},... | collective-permute-start | bytes 49160 | tf_op jit(solution)/shard_map/ppermute | solution.py:20
  132.6 4.9 %collective-permute-start.25 = (f32[4,8,1,128]{3,2,1,0:T(1,128)S(1)}, f32[4,8,1,128]{3,2,1,0:T(1,128)S(1)}, u32[]{:S(2)}, u32[]{:S(2)}) collective-permute-start(f32[4,8,1,128]{3,2,1,0:T(1,128)S(1)} %get-tuple-element.97), channel_id=1, source_target_pairs={{16,0},{32,16},{48,32},{64,48},{80,64},{96,80},{112,96},{128,112},... | collective-permute-start | bytes 49160 | tf_op jit(solution)/shard_map/ppermute | solution.py:22
  137.5 1.0 fusion.4
  139.1 2.5 %collective-permute-start.26 = (f32[4,8,10,1]{3,2,1,0:T(8,128)S(1)}, f32[4,8,10,1]{3,2,1,0:T(8,128)S(1)}, u32[]{:S(2)}, u32[]{:S(2)}) collective-permute-start(f32[4,8,10,1]{3,2,1,0:T(8,128)S(1)} %get-tuple-element.86), channel_id=1, source_target_pairs={{0,2},{2,4},{4,6},{6,8},{8,10},{10,12},{12,14},{1,3},{3,5},{5,7},{... | collective-permute-start | bytes 3848 | tf_op jit(solution)/shard_map/ppermute | solution.py:20
  141.6 1.3 collective-permute-start.27
  143.2 2.9 %collective-permute-start.31 = (f32[32]{0:T(128)S(1)}, f32[32]{0:T(128)S(1)}, u32[]{:S(2)}, u32[]{:S(2)}) collective-permute-start(f32[32]{0:T(128)S(1)} %get-tuple-element.7), channel_id=1, source_target_pairs={{16,0},{32,16},{48,32},{64,48},{80,64},{96,80},{112,96},{128,112},... | collective-permute-start | bytes 392 | tf_op jit(solution)/shard_map/ppermute | solution.py:32
  146.5 6.4 %collective-permute-done.27 = f32[4,8,10,1]{3,2,1,0:T(8,128)S(1)} collective-permute-done((f32[4,8,10,1]{3,2,1,0:T(8,128)S(1)}, f32[4,8,10,1]{3,2,1,0:T(8,128)S(1)}, u32[]{:S(2)}, u32[]{:S(2)}) %collective-permute-start.27) | collective-permute-done | bytes 1312 | tf_op jit(solution)/shard_map/ppermute | solution.py:22
  153.0 2.1 %collective-permute-start.28 = (f32[4,1,10,130]{3,2,1,0:T(8,128)S(1)}, f32[4,1,10,130]{3,2,1,0:T(8,128)S(1)}, u32[]{:S(2)}, u32[]{:S(2)}) collective-permute-start(f32[4,1,10,130]{3,2,1,0:T(8,128)S(1)} %get-tuple-element.58), channel_id=1, source_target_pairs={{0,1},{2,3},{4,5},{6,7},{8,9},{10,11},{12,13},{14,15},{16,17},{18,... | collective-permute-start | bytes 62408 | tf_op jit(solution)/shard_map/ppermute | solution.py:20
  155.0 1.3 collective-permute-start.29
  156.9 5.8 %collective-permute-done.29 = f32[4,1,10,130]{3,2,1,0:T(8,128)S(1)} collective-permute-done((f32[4,1,10,130]{3,2,1,0:T(8,128)S(1)}, f32[4,1,10,130]{3,2,1,0:T(8,128)S(1)}, u32[]{:S(2)}, u32[]{:S(2)}) %collective-permute-start.29) | collective-permute-done | bytes 20832 | tf_op jit(solution)/shard_map/ppermute | solution.py:22
  164.1 0.7 pad_maximum_fusion.10
  (98 shorter events, 12.7 us)
Async XLA Ops:
  0.6 1.8 %copy-start = (f32[16384]{0:T(1024)S(1)}, f32[16384]{0:T(1024)}, u32[]{:S(2)}) copy-start(f32[16384]{0:T(1024)} %param.11) | copy-start | bytes 196612
  3.3 0.9 copy-start.2
  3.3 7.7 %copy-start.1 = (f32[2,4,8,8,128]{4,3,2,1,0:T(8,128)S(1)}, f32[2,4,8,8,128]{4,3,2,1,0:T(8,128)}, u32[]{:S(2)}) copy-start(f32[2,4,8,8,128]{4,3,2,1,0:T(8,128)} %param.6) | copy-start | bytes 786436
  4.2 13.6 %collective-permute-start = (f32[4,8,1,128]{3,2,1,0:T(1,128)S(1)}, f32[4,8,1,128]{3,2,1,0:T(1,128)S(1)}, u32[]{:S(2)}, u32[]{:S(2)}) collective-permute-start(f32[4,8,1,128]{3,2,1,0:T(1,128)S(1)} %get-tuple-element.102), channel_id=1, source_target_pairs={{0,16},{16,32},{32,48},{48,64},{64,80},{80,96},{96,112},{112,128},... | collective-permute-start | bytes 49160 | tf_op jit(solution)/shard_map/ppermute | solution.py:20
  6.1 11.7 %collective-permute-start.1 = (f32[4,8,1,128]{3,2,1,0:T(1,128)S(1)}, f32[4,8,1,128]{3,2,1,0:T(1,128)S(1)}, u32[]{:S(2)}, u32[]{:S(2)}) collective-permute-start(f32[4,8,1,128]{3,2,1,0:T(1,128)S(1)} %get-tuple-element.103), channel_id=1, source_target_pairs={{16,0},{32,16},{48,32},{64,48},{80,64},{96,80},{112,96},{128,112},... | collective-permute-start | bytes 49160 | tf_op jit(solution)/shard_map/ppermute | solution.py:22
  11.0 11.7 %collective-permute-start.6 = (f32[4,8,1,128]{3,2,1,0:T(1,128)S(1)}, f32[4,8,1,128]{3,2,1,0:T(1,128)S(1)}, u32[]{:S(2)}, u32[]{:S(2)}) collective-permute-start(f32[4,8,1,128]{3,2,1,0:T(1,128)S(1)} %get-tuple-element.104), channel_id=1, source_target_pairs={{0,16},{16,32},{32,48},{48,64},{64,80},{80,96},{96,112},{112,128},... | collective-permute-start | bytes 49160 | tf_op jit(solution)/shard_map/ppermute | solution.py:20
  13.0 9.8 %collective-permute-start.7 = (f32[4,8,1,128]{3,2,1,0:T(1,128)S(1)}, f32[4,8,1,128]{3,2,1,0:T(1,128)S(1)}, u32[]{:S(2)}, u32[]{:S(2)}) collective-permute-start(f32[4,8,1,128]{3,2,1,0:T(1,128)S(1)} %get-tuple-element.105), channel_id=1, source_target_pairs={{16,0},{32,16},{48,32},{64,48},{80,64},{96,80},{112,96},{128,112},... | collective-permute-start | bytes 49160 | tf_op jit(solution)/shard_map/ppermute | solution.py:22
  18.0 10.8 %collective-permute-start.2 = (f32[4,8,10,1]{3,2,1,0:T(8,128)S(1)}, f32[4,8,10,1]{3,2,1,0:T(8,128)S(1)}, u32[]{:S(2)}, u32[]{:S(2)}) collective-permute-start(f32[4,8,10,1]{3,2,1,0:T(8,128)S(1)} %get-tuple-element.92), channel_id=1, source_target_pairs={{0,2},{2,4},{4,6},{6,8},{8,10},{10,12},{12,14},{1,3},{3,5},{5,7},{... | collective-permute-start | bytes 3848 | tf_op jit(solution)/shard_map/ppermute | solution.py:20
  21.5 14.3 %collective-permute-start.3 = (f32[4,8,10,1]{3,2,1,0:T(8,128)S(1)}, f32[4,8,10,1]{3,2,1,0:T(8,128)S(1)}, u32[]{:S(2)}, u32[]{:S(2)}) collective-permute-start(f32[4,8,10,1]{3,2,1,0:T(8,128)S(1)} %get-tuple-element.93), channel_id=1, source_target_pairs={{2,0},{4,2},{6,4},{8,6},{10,8},{12,10},{14,12},{3,1},{5,3},{7,5},{... | collective-permute-start | bytes 3848 | tf_op jit(solution)/shard_map/ppermute | solution.py:22
  23.0 19.2 %collective-permute-start.8 = (f32[4,8,10,1]{3,2,1,0:T(8,128)S(1)}, f32[4,8,10,1]{3,2,1,0:T(8,128)S(1)}, u32[]{:S(2)}, u32[]{:S(2)}) collective-permute-start(f32[4,8,10,1]{3,2,1,0:T(8,128)S(1)} %get-tuple-element.94), channel_id=1, source_target_pairs={{0,2},{2,4},{4,6},{6,8},{8,10},{10,12},{12,14},{1,3},{3,5},{5,7},{... | collective-permute-start | bytes 3848 | tf_op jit(solution)/shard_map/ppermute | solution.py:20
  27.5 17.0 %collective-permute-start.9 = (f32[4,8,10,1]{3,2,1,0:T(8,128)S(1)}, f32[4,8,10,1]{3,2,1,0:T(8,128)S(1)}, u32[]{:S(2)}, u32[]{:S(2)}) collective-permute-start(f32[4,8,10,1]{3,2,1,0:T(8,128)S(1)} %get-tuple-element.95), channel_id=1, source_target_pairs={{2,0},{4,2},{6,4},{8,6},{10,8},{12,10},{14,12},{3,1},{5,3},{7,5},{... | collective-permute-start | bytes 3848 | tf_op jit(solution)/shard_map/ppermute | solution.py:22
  36.0 15.0 %collective-permute-start.4 = (f32[4,1,10,130]{3,2,1,0:T(8,128)S(1)}, f32[4,1,10,130]{3,2,1,0:T(8,128)S(1)}, u32[]{:S(2)}, u32[]{:S(2)}) collective-permute-start(f32[4,1,10,130]{3,2,1,0:T(8,128)S(1)} %get-tuple-element.64), channel_id=1, source_target_pairs={{0,1},{2,3},{4,5},{6,7},{8,9},{10,11},{12,13},{14,15},{16,17},{18,... | collective-permute-start | bytes 62408 | tf_op jit(solution)/shard_map/ppermute | solution.py:20
  40.9 10.1 %collective-permute-start.5 = (f32[4,1,10,130]{3,2,1,0:T(8,128)S(1)}, f32[4,1,10,130]{3,2,1,0:T(8,128)S(1)}, u32[]{:S(2)}, u32[]{:S(2)}) collective-permute-start(f32[4,1,10,130]{3,2,1,0:T(8,128)S(1)} %get-tuple-element.65), channel_id=1, source_target_pairs={{1,0},{3,2},{5,4},{7,6},{9,8},{11,10},{13,12},{15,14},{17,16},{19,... | collective-permute-start | bytes 62408 | tf_op jit(solution)/shard_map/ppermute | solution.py:22
  44.7 6.8 %collective-permute-start.10 = (f32[4,1,10,130]{3,2,1,0:T(8,128)S(1)}, f32[4,1,10,130]{3,2,1,0:T(8,128)S(1)}, u32[]{:S(2)}, u32[]{:S(2)}) collective-permute-start(f32[4,1,10,130]{3,2,1,0:T(8,128)S(1)} %get-tuple-element.66), channel_id=1, source_target_pairs={{0,1},{2,3},{4,5},{6,7},{8,9},{10,11},{12,13},{14,15},{16,17},{18,... | collective-permute-start | bytes 62408 | tf_op jit(solution)/shard_map/ppermute | solution.py:20
  49.7 7.7 %collective-permute-start.11 = (f32[4,1,10,130]{3,2,1,0:T(8,128)S(1)}, f32[4,1,10,130]{3,2,1,0:T(8,128)S(1)}, u32[]{:S(2)}, u32[]{:S(2)}) collective-permute-start(f32[4,1,10,130]{3,2,1,0:T(8,128)S(1)} %get-tuple-element.67), channel_id=1, source_target_pairs={{1,0},{3,2},{5,4},{7,6},{9,8},{11,10},{13,12},{15,14},{17,16},{19,... | collective-permute-start | bytes 62408 | tf_op jit(solution)/shard_map/ppermute | solution.py:22
  58.8 6.8 %collective-permute-start.12 = (f32[4,8,1,128]{3,2,1,0:T(1,128)S(1)}, f32[4,8,1,128]{3,2,1,0:T(1,128)S(1)}, u32[]{:S(2)}, u32[]{:S(2)}) collective-permute-start(f32[4,8,1,128]{3,2,1,0:T(1,128)S(1)} %get-tuple-element.100), channel_id=1, source_target_pairs={{0,16},{16,32},{32,48},{48,64},{64,80},{80,96},{96,112},{112,128},... | collective-permute-start | bytes 49160 | tf_op jit(solution)/shard_map/ppermute | solution.py:20
  60.7 6.3 %collective-permute-start.13 = (f32[4,8,1,128]{3,2,1,0:T(1,128)S(1)}, f32[4,8,1,128]{3,2,1,0:T(1,128)S(1)}, u32[]{:S(2)}, u32[]{:S(2)}) collective-permute-start(f32[4,8,1,128]{3,2,1,0:T(1,128)S(1)} %get-tuple-element.101), channel_id=1, source_target_pairs={{16,0},{32,16},{48,32},{64,48},{80,64},{96,80},{112,96},{128,112},... | collective-permute-start | bytes 49160 | tf_op jit(solution)/shard_map/ppermute | solution.py:22
  67.2 8.9 %collective-permute-start.14 = (f32[4,8,10,1]{3,2,1,0:T(8,128)S(1)}, f32[4,8,10,1]{3,2,1,0:T(8,128)S(1)}, u32[]{:S(2)}, u32[]{:S(2)}) collective-permute-start(f32[4,8,10,1]{3,2,1,0:T(8,128)S(1)} %get-tuple-element.90), channel_id=1, source_target_pairs={{0,2},{2,4},{4,6},{6,8},{8,10},{10,12},{12,14},{1,3},{3,5},{5,7},{... | collective-permute-start | bytes 3848 | tf_op jit(solution)/shard_map/ppermute | solution.py:20
  70.0 14.6 %collective-permute-start.15 = (f32[4,8,10,1]{3,2,1,0:T(8,128)S(1)}, f32[4,8,10,1]{3,2,1,0:T(8,128)S(1)}, u32[]{:S(2)}, u32[]{:S(2)}) collective-permute-start(f32[4,8,10,1]{3,2,1,0:T(8,128)S(1)} %get-tuple-element.91), channel_id=1, source_target_pairs={{2,0},{4,2},{6,4},{8,6},{10,8},{12,10},{14,12},{3,1},{5,3},{7,5},{... | collective-permute-start | bytes 3848 | tf_op jit(solution)/shard_map/ppermute | solution.py:22
  84.8 3.5 %collective-permute-start.16 = (f32[4,1,10,130]{3,2,1,0:T(8,128)S(1)}, f32[4,1,10,130]{3,2,1,0:T(8,128)S(1)}, u32[]{:S(2)}, u32[]{:S(2)}) collective-permute-start(f32[4,1,10,130]{3,2,1,0:T(8,128)S(1)} %get-tuple-element.62), channel_id=1, source_target_pairs={{0,1},{2,3},{4,5},{6,7},{8,9},{10,11},{12,13},{14,15},{16,17},{18,... | collective-permute-start | bytes 62408 | tf_op jit(solution)/shard_map/ppermute | solution.py:20
  86.4 7.7 %collective-permute-start.17 = (f32[4,1,10,130]{3,2,1,0:T(8,128)S(1)}, f32[4,1,10,130]{3,2,1,0:T(8,128)S(1)}, u32[]{:S(2)}, u32[]{:S(2)}) collective-permute-start(f32[4,1,10,130]{3,2,1,0:T(8,128)S(1)} %get-tuple-element.63), channel_id=1, source_target_pairs={{1,0},{3,2},{5,4},{7,6},{9,8},{11,10},{13,12},{15,14},{17,16},{19,... | collective-permute-start | bytes 62408 | tf_op jit(solution)/shard_map/ppermute | solution.py:22
  95.5 6.8 %collective-permute-start.18 = (f32[4,8,1,128]{3,2,1,0:T(1,128)S(1)}, f32[4,8,1,128]{3,2,1,0:T(1,128)S(1)}, u32[]{:S(2)}, u32[]{:S(2)}) collective-permute-start(f32[4,8,1,128]{3,2,1,0:T(1,128)S(1)} %get-tuple-element.98), channel_id=1, source_target_pairs={{0,16},{16,32},{32,48},{48,64},{64,80},{80,96},{96,112},{112,128},... | collective-permute-start | bytes 49160 | tf_op jit(solution)/shard_map/ppermute | solution.py:20
  97.4 6.3 %collective-permute-start.19 = (f32[4,8,1,128]{3,2,1,0:T(1,128)S(1)}, f32[4,8,1,128]{3,2,1,0:T(1,128)S(1)}, u32[]{:S(2)}, u32[]{:S(2)}) collective-permute-start(f32[4,8,1,128]{3,2,1,0:T(1,128)S(1)} %get-tuple-element.99), channel_id=1, source_target_pairs={{16,0},{32,16},{48,32},{64,48},{80,64},{96,80},{112,96},{128,112},... | collective-permute-start | bytes 49160 | tf_op jit(solution)/shard_map/ppermute | solution.py:22
  103.9 7.2 %collective-permute-start.20 = (f32[4,8,10,1]{3,2,1,0:T(8,128)S(1)}, f32[4,8,10,1]{3,2,1,0:T(8,128)S(1)}, u32[]{:S(2)}, u32[]{:S(2)}) collective-permute-start(f32[4,8,10,1]{3,2,1,0:T(8,128)S(1)} %get-tuple-element.88), channel_id=1, source_target_pairs={{0,2},{2,4},{4,6},{6,8},{8,10},{10,12},{12,14},{1,3},{3,5},{5,7},{... | collective-permute-start | bytes 3848 | tf_op jit(solution)/shard_map/ppermute | solution.py:20
  106.4 12.9 %collective-permute-start.21 = (f32[4,8,10,1]{3,2,1,0:T(8,128)S(1)}, f32[4,8,10,1]{3,2,1,0:T(8,128)S(1)}, u32[]{:S(2)}, u32[]{:S(2)}) collective-permute-start(f32[4,8,10,1]{3,2,1,0:T(8,128)S(1)} %get-tuple-element.89), channel_id=1, source_target_pairs={{2,0},{4,2},{6,4},{8,6},{10,8},{12,10},{14,12},{3,1},{5,3},{7,5},{... | collective-permute-start | bytes 3848 | tf_op jit(solution)/shard_map/ppermute | solution.py:22
  119.5 3.3 %collective-permute-start.22 = (f32[4,1,10,130]{3,2,1,0:T(8,128)S(1)}, f32[4,1,10,130]{3,2,1,0:T(8,128)S(1)}, u32[]{:S(2)}, u32[]{:S(2)}) collective-permute-start(f32[4,1,10,130]{3,2,1,0:T(8,128)S(1)} %get-tuple-element.60), channel_id=1, source_target_pairs={{0,1},{2,3},{4,5},{6,7},{8,9},{10,11},{12,13},{14,15},{16,17},{18,... | collective-permute-start | bytes 62408 | tf_op jit(solution)/shard_map/ppermute | solution.py:20
  121.0 7.7 %collective-permute-start.23 = (f32[4,1,10,130]{3,2,1,0:T(8,128)S(1)}, f32[4,1,10,130]{3,2,1,0:T(8,128)S(1)}, u32[]{:S(2)}, u32[]{:S(2)}) collective-permute-start(f32[4,1,10,130]{3,2,1,0:T(8,128)S(1)} %get-tuple-element.61), channel_id=1, source_target_pairs={{1,0},{3,2},{5,4},{7,6},{9,8},{11,10},{13,12},{15,14},{17,16},{19,... | collective-permute-start | bytes 62408 | tf_op jit(solution)/shard_map/ppermute | solution.py:22
  129.5 1.0 copy-start.3
  130.7 7.8 %collective-permute-start.24 = (f32[4,8,1,128]{3,2,1,0:T(1,128)S(1)}, f32[4,8,1,128]{3,2,1,0:T(1,128)S(1)}, u32[]{:S(2)}, u32[]{:S(2)}) collective-permute-start(f32[4,8,1,128]{3,2,1,0:T(1,128)S(1)} %get-tuple-element.96), channel_id=1, source_target_pairs={{0,16},{16,32},{32,48},{48,64},{64,80},{80,96},{96,112},{112,128},... | collective-permute-start | bytes 49160 | tf_op jit(solution)/shard_map/ppermute | solution.py:20
  132.6 6.3 %collective-permute-start.25 = (f32[4,8,1,128]{3,2,1,0:T(1,128)S(1)}, f32[4,8,1,128]{3,2,1,0:T(1,128)S(1)}, u32[]{:S(2)}, u32[]{:S(2)}) collective-permute-start(f32[4,8,1,128]{3,2,1,0:T(1,128)S(1)} %get-tuple-element.97), channel_id=1, source_target_pairs={{16,0},{32,16},{48,32},{64,48},{80,64},{96,80},{112,96},{128,112},... | collective-permute-start | bytes 49160 | tf_op jit(solution)/shard_map/ppermute | solution.py:22
  138.5 4.4 %copy-start.4 = (s32[1,1,1,64]{3,2,1,0:T(1,128)S(1)}, s32[1,1,1,64]{3,2,1,0:T(1,128)}, u32[]{:S(2)}) copy-start(s32[1,1,1,64]{3,2,1,0:T(1,128)} %param.10) | copy-start | bytes 772
  139.1 7.4 %collective-permute-start.26 = (f32[4,8,10,1]{3,2,1,0:T(8,128)S(1)}, f32[4,8,10,1]{3,2,1,0:T(8,128)S(1)}, u32[]{:S(2)}, u32[]{:S(2)}) collective-permute-start(f32[4,8,10,1]{3,2,1,0:T(8,128)S(1)} %get-tuple-element.86), channel_id=1, source_target_pairs={{0,2},{2,4},{4,6},{6,8},{8,10},{10,12},{12,14},{1,3},{3,5},{5,7},{... | collective-permute-start | bytes 3848 | tf_op jit(solution)/shard_map/ppermute | solution.py:20
  141.6 11.2 %collective-permute-start.27 = (f32[4,8,10,1]{3,2,1,0:T(8,128)S(1)}, f32[4,8,10,1]{3,2,1,0:T(8,128)S(1)}, u32[]{:S(2)}, u32[]{:S(2)}) collective-permute-start(f32[4,8,10,1]{3,2,1,0:T(8,128)S(1)} %get-tuple-element.87), channel_id=1, source_target_pairs={{2,0},{4,2},{6,4},{8,6},{10,8},{12,10},{14,12},{3,1},{5,3},{7,5},{... | collective-permute-start | bytes 3848 | tf_op jit(solution)/shard_map/ppermute | solution.py:22
  143.1 13.2 %collective-permute-start.30 = (f32[32]{0:T(128)S(1)}, f32[32]{0:T(128)S(1)}, u32[]{:S(2)}, u32[]{:S(2)}) collective-permute-start(f32[32]{0:T(128)S(1)} %get-tuple-element.6), channel_id=1, source_target_pairs={{496,0},{0,16},{16,32},{32,48},{48,64},{64,80},{80,96},{96,112},{1... | collective-permute-start | bytes 392 | tf_op jit(solution)/shard_map/ppermute | solution.py:32
  143.2 13.2 %collective-permute-start.31 = (f32[32]{0:T(128)S(1)}, f32[32]{0:T(128)S(1)}, u32[]{:S(2)}, u32[]{:S(2)}) collective-permute-start(f32[32]{0:T(128)S(1)} %get-tuple-element.7), channel_id=1, source_target_pairs={{16,0},{32,16},{48,32},{64,48},{80,64},{96,80},{112,96},{128,112},... | collective-permute-start | bytes 392 | tf_op jit(solution)/shard_map/ppermute | solution.py:32
  153.0 3.9 %collective-permute-start.28 = (f32[4,1,10,130]{3,2,1,0:T(8,128)S(1)}, f32[4,1,10,130]{3,2,1,0:T(8,128)S(1)}, u32[]{:S(2)}, u32[]{:S(2)}) collective-permute-start(f32[4,1,10,130]{3,2,1,0:T(8,128)S(1)} %get-tuple-element.58), channel_id=1, source_target_pairs={{0,1},{2,3},{4,5},{6,7},{8,9},{10,11},{12,13},{14,15},{16,17},{18,... | collective-permute-start | bytes 62408 | tf_op jit(solution)/shard_map/ppermute | solution.py:20
  155.0 7.7 %collective-permute-start.29 = (f32[4,1,10,130]{3,2,1,0:T(8,128)S(1)}, f32[4,1,10,130]{3,2,1,0:T(8,128)S(1)}, u32[]{:S(2)}, u32[]{:S(2)}) collective-permute-start(f32[4,1,10,130]{3,2,1,0:T(8,128)S(1)} %get-tuple-element.59), channel_id=1, source_target_pairs={{1,0},{3,2},{5,4},{7,6},{9,8},{11,10},{13,12},{15,14},{17,16},{19,... | collective-permute-start | bytes 62408 | tf_op jit(solution)/shard_map/ppermute | solution.py:22
where the time goes:
time: 166 us; the launch traced here: 165 us
  starting transfers between devices  80.5 us (48%)
  waiting for transfers between devices  68.7 us (41%)
  other arithmetic  9.99 us (6%)
  local copies, waits for them, and re-layouts  2.53 us (2%)
    ppermute x15, waiting for transfers between devices, padded(): lax.ppermute(head, axis, [((i + 1) % count, i) for i in range(ends)])  58.8 us
    ppermute x15, starting transfers between devices, padded(): lax.ppermute(tail, axis, [(i, (i + 1) % count) for i in range(ends)])  40.4 us
    ppermute x15, starting transfers between devices, padded(): lax.ppermute(head, axis, [((i + 1) % count, i) for i in range(ends)])  37.2 us
    ppermute x15, waiting for transfers between devices, padded(): lax.ppermute(tail, axis, [(i, (i + 1) % count) for i in range(ends)])  9.95 us
  transfers between devices with their start and end apart: 32, of which 18 were waited for; matrix products, arithmetic and copies ran while one was open for 2% of the time, Pallas kernels for 0%

commit v1 on v0

v1 whole, which is shorter than its diff:
```python
import functools

import jax
import jax.numpy as jnp
from jax import lax
from jax.experimental import pallas as pl
from jax.experimental.pallas import tpu as pltpu
from jax.sharding import PartitionSpec as P

FAC_DEV = 32
TIME_STEP = 0.3
HALF = TIME_STEP
FULL = 2.0 * TIME_STEP
MESH = pl.DeviceIdType.MESH
F32 = jnp.float32


def kernel(sizes, steps, adj, saved, wind, slot, table, imp, out, grad,
           mid, upp, sav, win, slo, tab, damp, part, prod, flux_z,
           xs, ys, zs, xr, yr, zr, smat, gs, gr,
           in_sem, x_ss, x_rs, y_ss, y_rs, z_ss, z_rs, g_ss, g_rs):
    nx, ny, nz = sizes
    ix, iy, iz = lax.axis_index("gx"), lax.axis_index("gy"), lax.axis_index("gz")
    right = (lax.rem(ix + 1, nx), iy, iz)
    left = (lax.rem(ix + nx - 1, nx), iy, iz)
    north = (ix, lax.rem(iy + 1, ny), iz)
    south = (ix, lax.rem(iy + ny - 1, ny), iz)
    other = (ix, iy, 1 - iz)
    barrier = pltpu.get_barrier_semaphore()
    for dev in (left, right, south, north, other):
        pl.semaphore_signal(barrier, inc=1, device_id=dev, device_id_type=MESH)

    loads = []
    for i, (src, dst) in enumerate(
        [(wind, win), (adj.at[1], mid), (table, tab), (slot, slo), (adj.at[0], upp), (saved, sav)]
    ):
        copy = pltpu.make_async_copy(src, dst, in_sem.at[i])
        copy.start()
        loads.append(copy)

    lane = lax.broadcasted_iota(jnp.int32, (8, 128), 1)
    row = lax.broadcasted_iota(jnp.int32, (8, 128), 0)
    first_row, last_row = row == 0, row == 7
    first_lane, last_lane = lane == 0, lane == 127
    odd = lax.rem(lane, 2) == 1

    def fluxes(c, s, w0, w1, w2):
        own = s[c]
        fz, fx, fy = w0 * own, w1 * own, w2 * own
        if c == 0:
            fz, fx, fy = fz + s[1], fx + s[2], fy + s[3]
        elif c == 1:
            fz = fz + s[0]
        elif c == 2:
            fx = fx + s[0]
        else:
            fy = fy + s[0]
        return fz, fx, fy

    def faces(k, m):
        low = jnp.zeros((8, 128), F32)
        high = jnp.zeros((8, 128), F32)
        allf = [[None] * 8 for _ in range(4)]
        for z in range(8):
            w0, w1, w2 = win[0, z], win[1, z], win[2, z]
            s = [m[c][z] for c in range(4)]
            for c in range(4):
                fz, fx, fy = fluxes(c, s, w0, w1, w2)
                allf[c][z] = (fz, fx, fy)
                n = c * 8 + z
                xs[k, 0, pl.ds(n, 1), :] = fx[0:1]
                xs[k, 1, pl.ds(n, 1), :] = fx[7:8]
                p = 2 * n + 1
                moved = pltpu.roll(fy, p + 1, 1)
                high = jnp.where(lane == p, moved, high)
                low = jnp.where(lane == p + 1, moved, low)
        ys[k, 0] = low
        ys[k, 1] = high
        for c in range(4):
            zs[k, c] = jnp.where(iz == 0, allf[c][7][0], allf[c][0][0])
        return allf

    def copies(k):
        mk = pltpu.make_async_remote_copy
        return [
            mk(src_ref=ys.at[k, 1], dst_ref=yr.at[k, 0], send_sem=y_ss.at[k, 0], recv_sem=y_rs.at[k, 0], device_id=north, device_id_type=MESH),
            mk(src_ref=ys.at[k, 0], dst_ref=yr.at[k, 1], send_sem=y_ss.at[k, 1], recv_sem=y_rs.at[k, 1], device_id=south, device_id_type=MESH),
            mk(src_ref=zs.at[k], dst_ref=zr.at[k], send_sem=z_ss.at[k], recv_sem=z_rs.at[k], device_id=other, device_id_type=MESH),
            mk(src_ref=xs.at[k, 1], dst_ref=xr.at[k, 0], send_sem=x_ss.at[k, 0], recv_sem=x_rs.at[k, 0], device_id=right, device_id_type=MESH),
            mk(src_ref=xs.at[k, 0], dst_ref=xr.at[k, 1], send_sem=x_ss.at[k, 1], recv_sem=x_rs.at[k, 1], device_id=left, device_id_type=MESH),
        ]

    def inner(m, allf, upper):
        for z in range(8):
            d = damp[z] * FULL
            for c in range(4):
                fz, fx, fy = allf[c][z]
                dx = jnp.where(last_row, 0.0, pltpu.roll(fx, 7, 0)) - jnp.where(first_row, 0.0, pltpu.roll(fx, 1, 0))
                dy = jnp.where(last_lane, 0.0, pltpu.roll(fy, 127, 1)) - jnp.where(first_lane, 0.0, pltpu.roll(fy, 1, 1))
                total = dx + dy
                if z < 7:
                    total = total + allf[c][z + 1][0]
                if z > 0:
                    total = total - allf[c][z - 1][0]
                part[c, z] = upper[c][z] + HALF * total - d * m[c][z]

    def finish(k):
        low = jnp.where(iy > 0, -yr[k, 0], 0.0)
        high = jnp.where(iy < ny - 1, pltpu.roll(yr[k, 1], 126, 1), 0.0)
        both = HALF * jnp.where(odd, low, high)
        from_left = jnp.where(ix > 0, -HALF, 0.0)
        from_right = jnp.where(ix < nx - 1, HALF, 0.0)
        top = jnp.where(iz == 0, HALF, 0.0)
        bottom = jnp.where(iz == 0, 0.0, HALF)
        m = [[None] * 8 for _ in range(4)]
        for z in range(8):
            for c in range(4):
                n = c * 8 + z
                value = part[c, z]
                edge = pltpu.roll(both, 128 - (2 * n + 1), 1)
                value = value + jnp.where(first_lane | last_lane, edge, 0.0)
                lrow = xr[k, 0, pl.ds(n, 1), :] * from_left
                rrow = xr[k, 1, pl.ds(n, 1), :] * from_right
                value = value + jnp.where(first_row, lrow, jnp.where(last_row, rrow, 0.0))
                if z == 7:
                    value = value + top * zr[k, c]
                if z == 0:
                    value = value - bottom * zr[k, c]
                m[c][z] = value
        return m

    def add_products(k, m):
        for z in range(8):
            total = m[0][z] * sav[k, 0, z]
            for c in range(1, 4):
                total = total + m[c][z] * sav[k, c, z]
            prod[z] = total if k == 0 else prod[z] + total

    loads[0].wait()
    loads[1].wait()
    m = [[mid[c, z] for z in range(8)] for c in range(4)]
    allf = faces(0, m)
    pl.semaphore_wait(barrier, 5)
    sends = copies(0)
    for copy in sends:
        copy.start()
    everything = list(sends)

    loads[2].wait()
    loads[3].wait()
    group = iy * nz + iz
    per_row = 128 // FAC_DEV
    stride = (ny * nz) // per_row
    row_of = [lax.rem(ix + o + nx, nx) * stride + group // per_row for o in (0, 1, -1)]
    ids = jnp.broadcast_to(tab[...], (8, 128))
    id_row = lax.shift_right_logical(ids, 7)
    id_lane = jnp.bitwise_and(ids, 127)
    lut = jnp.zeros((8, 128), F32)
    for o in range(3):
        line = jnp.broadcast_to(imp[pl.ds(row_of[o], 1), :], (8, 128))
        lut = jnp.where(id_row == row_of[o], jnp.take_along_axis(line, id_lane, axis=1), lut)
    place = jnp.where(id_row == row_of[0], 0, jnp.where(id_row == row_of[1], 32, 64)) + jnp.bitwise_and(ids, 31)
    for z in range(8):
        names = slo[z]
        value = jnp.take_along_axis(lut, jnp.maximum(names - 1, 0), axis=1)
        damp[z] = jnp.where(names > 0, value, 0.0)

    loads[4].wait()
    inner(m, allf, [[upp[c, z] for z in range(8)] for c in range(4)])
    loads[5].wait()
    add_products(0, m)

    older = m
    for k in range(steps):
        for copy in sends:
            copy.wait_recv()
        new = finish(k)
        if k == steps - 1:
            for c in range(4):
                for z in range(8):
                    out[1, c, z] = new[c][z]
            break
        for c in range(4):
            for z in range(8):
                if k == steps - 2:
                    out[0, c, z] = new[c][z]
        allf = faces(k + 1, new)
        sends = copies(k + 1)
        for copy in sends:
            copy.start()
        everything += sends
        add_products(k + 1, new)
        if k == steps - 2:
            for s in range(64):
                total = jnp.zeros((8, 128), F32)
                for z in range(8):
                    total = total + jnp.where(slo[z] == s + 1, prod[z], 0.0)
                smat[pl.ds(s, 1), :] = jnp.sum(total, axis=0, keepdims=True)
            sums = jnp.sum(smat[...], axis=1, keepdims=True) * (-FULL)
            turned = jnp.transpose(jnp.broadcast_to(place[0:1], (128, 128)))[0:64]
            wide = lax.broadcasted_iota(jnp.int32, (64, 128), 1)
            facades = jnp.sum(jnp.where(turned == wide, sums, 0.0), axis=0, keepdims=True)
            gs[...] = jnp.broadcast_to(facades, (8, 128))
            g_sends = [
                pltpu.make_async_remote_copy(src_ref=gs, dst_ref=gr.at[0], send_sem=g_ss.at[0], recv_sem=g_rs.at[0], device_id=right, device_id_type=MESH),
                pltpu.make_async_remote_copy(src_ref=gs, dst_ref=gr.at[1], send_sem=g_ss.at[1], recv_sem=g_rs.at[1], device_id=left, device_id_type=MESH),
            ]
            for copy in g_sends:
                copy.start()
        inner(new, allf, older)
        older = new
    for copy in g_sends:
        copy.wait_recv()
    total = gs[...] + pltpu.roll(gr[0], 96, 1) + pltpu.roll(gr[1], 64, 1)
    grad[...] = total[0:1]
    for copy in everything + g_sends:
        copy.wait_send()


def local(sizes, adjoint, saved_state, wind_field, facade_slot, facade_table, impedance):
    steps = saved_state.shape[0]
    table = jnp.pad(facade_table.reshape(1, -1), ((0, 0), (0, 64)))
    imp = impedance.reshape(-1, 128)
    any_spec = pl.BlockSpec(memory_space=pl.ANY)
    vmem_spec = pl.BlockSpec(memory_space=pltpu.VMEM)
    v = pltpu.VMEM
    dma = pltpu.SemaphoreType.DMA
    out, grad = pl.pallas_call(
        functools.partial(kernel, sizes, steps),
        out_shape=[
            jax.ShapeDtypeStruct(adjoint.shape, F32),
            jax.ShapeDtypeStruct((1, 128), F32),
        ],
        in_specs=[any_spec] * 5 + [vmem_spec],
        out_specs=[vmem_spec, vmem_spec],
        scratch_shapes=[
            v((4, 8, 8, 128), F32),
            v((4, 8, 8, 128), F32),
            v((steps, 4, 8, 8, 128), F32),
            v((3, 8, 8, 128), F32),
            v((8, 8, 128), jnp.int32),
            v((1, 128), jnp.int32),
            v((8, 8, 128), F32),
            v((4, 8, 8, 128), F32),
            v((8, 8, 128), F32),
            v((8, 128), F32),
            v((steps, 2, 32, 128), F32),
            v((steps, 2, 8, 128), F32),
            v((steps, 4, 8, 128), F32),
            v((steps, 2, 32, 128), F32),
            v((steps, 2, 8, 128), F32),
            v((steps, 4, 8, 128), F32),
            v((64, 128), F32),
            v((8, 128), F32),
            v((2, 8, 128), F32),
            dma((6,)),
            dma((steps, 2)), dma((steps, 2)), dma((steps, 2)), dma((steps, 2)),
            dma((steps,)), dma((steps,)), dma((2,)), dma((2,)),
        ],
        compiler_params=pltpu.CompilerParams(
            collective_id=0, has_side_effects=True, vmem_limit_bytes=32 << 20
        ),
    )(adjoint, saved_state, wind_field, facade_slot, table, imp)
    return out, grad[0, :FAC_DEV]


def solution(mesh):
    sizes = tuple(mesh.shape[a] for a in ("gx", "gy", "gz"))
    return jax.shard_map(
        functools.partial(local, sizes),
        mesh=mesh,
        in_specs=(
            P(None, None, "gz", "gx", "gy"),
            P(None, None, "gz", "gx", "gy"),
            P(None, "gz", "gx", "gy"),
            P("gz", "gx", "gy"),
            P("gz", "gx", "gy", None),
            P(),
        ),
        out_specs=(P(None, None, "gz", "gx", "gy"), P(("gx", "gy", "gz"))),
        check_vma=False,
    )
```

time: 166 us -> 34.4 us (0.21)
  the two profiles are of different devices: /device:TPU:128 before, /device:TPU:4 now
where the time goes in v1:
time: 34.4 us; the launch traced here: 34.1 us
  Pallas kernels  27.1 us (79%)
  local copies, waits for them, and re-layouts  6.35 us (18%)
  between operations  0.65 us (2%)
    pallas_call x1, Pallas kernels, local(): pl.pallas_call(functools.partial(kernel, sizes, steps), out_shape=[jax.Sh...  27.1 us
    unnamed x13, local copies, waits for them, and re-layouts  5.83 us

profile of v1, /device:TPU:4, one launch (start us, length us, event | category | flops | bytes accessed | tf_op | source)
XLA Modules:
  0.0 34.1 jit_solution(2588900548549379180)
XLA Ops:
  0.6 0.0 copy-start.5
  0.6 0.6 %copy-done.5 = s32[1,1,1,64]{3,2,1,0:T(1,128)S(1)} copy-done((s32[1,1,1,64]{3,2,1,0:T(1,128)S(1)}, s32[1,1,1,64]{3,2,1,0:T(1,128)}, u32[]{:S(2)}) %copy-start.5) | copy-done | bytes 280
  1.3 0.0 copy-start
  1.3 1.0 %copy-done = f32[4,4,8,8,128]{4,3,2,1,0:T(8,128)S(1)} copy-done((f32[4,4,8,8,128]{4,3,2,1,0:T(8,128)S(1)}, f32[4,4,8,8,128]{4,3,2,1,0:T(8,128)}, u32[]{:S(2)}) %copy-start) | copy-done | bytes 524312
  2.3 0.0 copy-start.1
  2.3 0.9 %copy-done.1 = f32[2,4,8,8,128]{4,3,2,1,0:T(8,128)S(1)} copy-done((f32[2,4,8,8,128]{4,3,2,1,0:T(8,128)S(1)}, f32[2,4,8,8,128]{4,3,2,1,0:T(8,128)}, u32[]{:S(2)}) %copy-start.1) | copy-done | bytes 262168
  3.3 0.0 copy-start.2
  3.3 0.9 %copy-done.2 = f32[3,8,8,128]{3,2,1,0:T(8,128)S(1)} copy-done((f32[3,8,8,128]{3,2,1,0:T(8,128)S(1)}, f32[3,8,8,128]{3,2,1,0:T(8,128)}, u32[]{:S(2)}) %copy-start.2) | copy-done | bytes 98328
  4.2 0.0 copy-start.3
  4.2 0.8 %copy-done.3 = f32[16384]{0:T(1024)S(1)} copy-done((f32[16384]{0:T(1024)S(1)}, f32[16384]{0:T(1024)}, u32[]{:S(2)}) %copy-start.3) | copy-done | bytes 65560
  5.0 0.0 copy-start.4
  5.0 0.8 %copy-done.4 = s32[8,8,128]{2,1,0:T(8,128)S(1)} copy-done((s32[8,8,128]{2,1,0:T(8,128)S(1)}, s32[8,8,128]{2,1,0:T(8,128)}, u32[]{:S(2)}) %copy-start.4) | copy-done | bytes 32792
  5.8 27.1 %shard_map.77 = (f32[2,4,8,8,128]{4,3,2,1,0:T(8,128)S(1)}, f32[1,128]{1,0:T(1,128)S(1)}) custom-call(f32[2,4,8,8,128]{4,3,2,1,0:T(8,128)S(1)} %copy-done.1, f32[4,4,8,8,128]{4,3,2,1,0:T(8,128)S(1)} %copy-done, f32[3,8,8,128]{3,2,1,0:T(8,128)S(1)} %copy-done.2, s32[8,8,128]{2,1,0:T(8,128)S(1)} %copy-done.4, s32[1,128]{1,0:T(1,128)S(1)} %pad.4.table, ...), custom_call_target="tpu_custom_call" | custom-call | tf_op jit(solution)/shard_map/pallas_call | solution.py:228
  32.9 0.5 %slice_bitcast_fusion = f32[32]{0:T(128)} fusion(f32[1,128]{1,0:T(1,128)S(1)} %get-tuple-element.5), kind=kLoop, calls=%fused_computation | loop fusion | bytes 256 | tf_op jit(solution)/shard_map/squeeze | solution.py:264
  33.4 0.7 %copy.9 = f32[2,4,8,8,128]{4,3,2,1,0:T(8,128)} copy(f32[2,4,8,8,128]{4,3,2,1,0:T(8,128)S(1)} %get-tuple-element.8) | data formatting | bytes 524288
  (1 shorter events, 0.0 us)
Async XLA Ops:
  0.6 0.7 %copy-start.5 = (s32[1,1,1,64]{3,2,1,0:T(1,128)S(1)}, s32[1,1,1,64]{3,2,1,0:T(1,128)}, u32[]{:S(2)}) copy-start(s32[1,1,1,64]{3,2,1,0:T(1,128)} %param.10) | copy-start | bytes 772
  1.3 1.0 %copy-start = (f32[4,4,8,8,128]{4,3,2,1,0:T(8,128)S(1)}, f32[4,4,8,8,128]{4,3,2,1,0:T(8,128)}, u32[]{:S(2)}) copy-start(f32[4,4,8,8,128]{4,3,2,1,0:T(8,128)} %saved.1) | copy-start | bytes 1572868
  2.3 0.9 %copy-start.1 = (f32[2,4,8,8,128]{4,3,2,1,0:T(8,128)S(1)}, f32[2,4,8,8,128]{4,3,2,1,0:T(8,128)}, u32[]{:S(2)}) copy-start(f32[2,4,8,8,128]{4,3,2,1,0:T(8,128)} %adj.1) | copy-start | bytes 786436
  3.3 0.9 %copy-start.2 = (f32[3,8,8,128]{3,2,1,0:T(8,128)S(1)}, f32[3,8,8,128]{3,2,1,0:T(8,128)}, u32[]{:S(2)}) copy-start(f32[3,8,8,128]{3,2,1,0:T(8,128)} %wind.1) | copy-start | bytes 294916
  4.2 0.8 %copy-start.3 = (f32[16384]{0:T(1024)S(1)}, f32[16384]{0:T(1024)}, u32[]{:S(2)}) copy-start(f32[16384]{0:T(1024)} %param.11) | copy-start | bytes 196612
  5.0 0.8 %copy-start.4 = (s32[8,8,128]{2,1,0:T(8,128)S(1)}, s32[8,8,128]{2,1,0:T(8,128)}, u32[]{:S(2)}) copy-start(s32[8,8,128]{2,1,0:T(8,128)} %slot.1) | copy-start | bytes 98308

commit v2 on v1

--- a/solution.py
+++ b/solution.py
@@ -15,8 +15,8 @@
 F32 = jnp.float32
 
 
-def kernel(sizes, steps, adj, saved, wind, slot, table, imp, out, grad,
-           mid, upp, sav, win, slo, tab, damp, part, prod, flux_z,
+def kernel(sizes, steps, adj, saved, wind, slot, table, impedance, out, grad,
+           mid, upp, sav, win, slo, tab, imp, damp, part, prod,
            xs, ys, zs, xr, yr, zr, smat, gs, gr,
            in_sem, x_ss, x_rs, y_ss, y_rs, z_ss, z_rs, g_ss, g_rs):
     nx, ny, nz = sizes
@@ -32,7 +32,8 @@
 
     loads = []
     for i, (src, dst) in enumerate(
-        [(wind, win), (adj.at[1], mid), (table, tab), (slot, slo), (adj.at[0], upp), (saved, sav)]
+        [(wind, win), (adj.at[1], mid), (table.at[0, 0], tab), (slot, slo), (impedance, imp),
+         (adj.at[0], upp), (saved, sav)]
     ):
         copy = pltpu.make_async_copy(src, dst, in_sem.at[i])
         copy.start()
@@ -148,11 +149,12 @@
 
     loads[2].wait()
     loads[3].wait()
+    loads[4].wait()
     group = iy * nz + iz
     per_row = 128 // FAC_DEV
     stride = (ny * nz) // per_row
     row_of = [lax.rem(ix + o + nx, nx) * stride + group // per_row for o in (0, 1, -1)]
-    ids = jnp.broadcast_to(tab[...], (8, 128))
+    ids = jnp.broadcast_to(jnp.concatenate([tab[...], tab[...]], axis=1), (8, 128))
     id_row = lax.shift_right_logical(ids, 7)
     id_lane = jnp.bitwise_and(ids, 127)
     lut = jnp.zeros((8, 128), F32)
@@ -165,9 +167,9 @@
         value = jnp.take_along_axis(lut, jnp.maximum(names - 1, 0), axis=1)
         damp[z] = jnp.where(names > 0, value, 0.0)
 
-    loads[4].wait()
+    loads[5].wait()
     inner(m, allf, [[upp[c, z] for z in range(8)] for c in range(4)])
-    loads[5].wait()
+    loads[6].wait()
     add_products(0, m)
 
     older = m
@@ -212,16 +214,15 @@
     for copy in g_sends:
         copy.wait_recv()
     total = gs[...] + pltpu.roll(gr[0], 96, 1) + pltpu.roll(gr[1], 64, 1)
-    grad[...] = total[0:1]
+    grad[...] = total[0, 0:FAC_DEV]
     for copy in everything + g_sends:
         copy.wait_send()
 
 
 def local(sizes, adjoint, saved_state, wind_field, facade_slot, facade_table, impedance):
     steps = saved_state.shape[0]
-    table = jnp.pad(facade_table.reshape(1, -1), ((0, 0), (0, 64)))
     imp = impedance.reshape(-1, 128)
-    any_spec = pl.BlockSpec(memory_space=pl.ANY)
+    hbm_spec = pl.BlockSpec(memory_space=pltpu.HBM)
     vmem_spec = pl.BlockSpec(memory_space=pltpu.VMEM)
     v = pltpu.VMEM
     dma = pltpu.SemaphoreType.DMA
@@ -229,9 +230,9 @@
         functools.partial(kernel, sizes, steps),
         out_shape=[
             jax.ShapeDtypeStruct(adjoint.shape, F32),
-            jax.ShapeDtypeStruct((1, 128), F32),
+            jax.ShapeDtypeStruct((FAC_DEV,), F32),
         ],
-        in_specs=[any_spec] * 5 + [vmem_spec],
+        in_specs=[hbm_spec] * 6,
         out_specs=[vmem_spec, vmem_spec],
         scratch_shapes=[
             v((4, 8, 8, 128), F32),
@@ -239,11 +240,11 @@
             v((steps, 4, 8, 8, 128), F32),
             v((3, 8, 8, 128), F32),
             v((8, 8, 128), jnp.int32),
-            v((1, 128), jnp.int32),
+            v((1, 64), jnp.int32),
+            v((128, 128), F32),
             v((8, 8, 128), F32),
             v((4, 8, 8, 128), F32),
             v((8, 8, 128), F32),
-            v((8, 128), F32),
             v((steps, 2, 32, 128), F32),
             v((steps, 2, 8, 128), F32),
             v((steps, 4, 8, 128), F32),
@@ -253,15 +254,16 @@
             v((64, 128), F32),
             v((8, 128), F32),
             v((2, 8, 128), F32),
-            dma((6,)),
+            dma((7,)),
             dma((steps, 2)), dma((steps, 2)), dma((steps, 2)), dma((steps, 2)),
             dma((steps,)), dma((steps,)), dma((2,)), dma((2,)),
         ],
         compiler_params=pltpu.CompilerParams(
             collective_id=0, has_side_effects=True, vmem_limit_bytes=32 << 20
         ),
-    )(adjoint, saved_state, wind_field, facade_slot, table, imp)
-    return out, grad[0, :FAC_DEV]
+    )(*[pltpu.with_memory_space_constraint(a, pltpu.HBM)
+        for a in (adjoint, saved_state, wind_field, facade_slot, facade_table, imp)])
+    return out, grad
 
 
 def solution(mesh):

time: 34.4 us -> 29.1 us (0.85)
  local copies, waits for them, and re-layouts: 6.35 us -> 1.22 us
    unnamed x13 -> x2, local copies, waits for them, and re-layouts: 5.83 us -> 1.22 us
    squeeze x1 -> x0, local copies, waits for them, and re-layouts: 0.51 us -> none  [local(): return (out, grad[0, :FAC_DEV])]
where the time goes in v2:
time: 29.1 us; the launch traced here: 29 us
  Pallas kernels  27.1 us (93%)
  local copies, waits for them, and re-layouts  1.22 us (4%)
  between operations  0.64 us (2%)
    pallas_call x1, Pallas kernels, local(): pl.pallas_call(functools.partial(kernel, sizes, steps), out_shape=[jax.Sh...  27.1 us
    unnamed x2, local copies, waits for them, and re-layouts  1.22 us

profile of v2, /device:TPU:4, one launch (start us, length us, event | category | flops | bytes accessed | tf_op | source)
XLA Modules:
  0.0 29.0 jit_solution(7885454382906188726)
XLA Ops:
  0.6 27.1 %shard_map.77 = (f32[2,4,8,8,128]{4,3,2,1,0:T(8,128)S(1)}, f32[32]{0:T(128)S(1)}) custom-call(f32[2,4,8,8,128]{4,3,2,1,0:T(8,128)} %adj.1, f32[4,4,8,8,128]{4,3,2,1,0:T(8,128)} %saved.1, f32[3,8,8,128]{3,2,1,0:T(8,128)} %wind.1, s32[8,8,128]{2,1,0:T(8,128)} %slot.1, s32[1,1,1,64]{3,2,1,0:T(1,128)} %table.1, f32[128,128]{1,0:T(8,128)} %bitcast.1), custom_call_target="tpu_custom_call" | custom-call | tf_op jit(solution)/shard_map/pallas_call | solution.py:229
  27.7 0.7 %copy.10 = f32[2,4,8,8,128]{4,3,2,1,0:T(8,128)} copy(f32[2,4,8,8,128]{4,3,2,1,0:T(8,128)S(1)} %get-tuple-element.4) | data formatting | bytes 524288
  28.5 0.5 %copy.11 = f32[32]{0:T(128)} copy(f32[32]{0:T(128)S(1)} %get-tuple-element.5) | data formatting | bytes 256

commit v3 on v0

v3 whole, which is shorter than its diff:
```python
import functools

import jax
import jax.numpy as jnp
from jax import lax
from jax.experimental import pallas as pl
from jax.experimental.pallas import tpu as pltpu
from jax.sharding import PartitionSpec as P

FAC_DEV = 32
TIME_STEP = 0.3
HALF = TIME_STEP
FULL = 2.0 * TIME_STEP
MESH = pl.DeviceIdType.MESH
F32 = jnp.float32

WIND, DAMP, FIELDS = 8, 11, 12
OWN, XH, YH, XYH = 0, 1, 2, 3


def when(cond, run):
    if cond is None:
        run()
    else:
        pl.when(cond)(run)


class Sent:
    def __init__(self, src, dst, send_sem, recv_sem, to, send_if=None, recv_if=None):
        self.copy = pltpu.make_async_remote_copy(
            src_ref=src, dst_ref=dst, send_sem=send_sem, recv_sem=recv_sem, device_id=to, device_id_type=MESH
        )
        self.send_if, self.recv_if = send_if, recv_if

    def start(self):
        when(self.send_if, self.copy.start)

    def wait_recv(self):
        when(self.recv_if, self.copy.wait_recv)

    def wait_send(self):
        when(self.send_if, self.copy.wait_send)


def kernel(sizes, adj, saved, wind, slot, table, impedance, out, grad,
           mid, upp, sav, win, slo, tab, imp, ext, part, prod,
           xbuf, ybuf, zbuf, xr, xzr, yr, yzr, zr, xyr, xyzr,
           xs, ys, zs, xf, yf, zf, smat, gs, gr,
           in_sem, ss, rs, fs, fr, g_ss, g_rs):
    nx, ny, nz = sizes
    ix, iy, iz = lax.axis_index("gx"), lax.axis_index("gy"), lax.axis_index("gz")
    has_right, has_left = ix < nx - 1, ix > 0

    def device(dx, dy, dz):
        return (
            lax.rem(ix + dx + nx, nx) if dx else ix,
            lax.rem(iy + dy + ny, ny) if dy else iy,
            1 - iz if dz else iz,
        )

    barrier = pltpu.get_barrier_semaphore()
    for dx in (0, 1, -1):
        def greet(dx=dx):
            for dy in (0, 1, -1):
                for dz in (1, 0):
                    if dx or dy or dz:
                        pl.semaphore_signal(barrier, inc=1, device_id=device(dx, dy, dz), device_id_type=MESH)

        when({0: None, 1: has_right, -1: has_left}[dx], greet)

    loads = []
    for i, (src, dst) in enumerate(
        [(table.at[0, 0], tab), (impedance, imp), (slot, slo), (wind, win), (adj.at[1], mid), (adj.at[0], upp), (saved, sav)]
    ):
        copy = pltpu.make_async_copy(src, dst, in_sem.at[i])
        copy.start()
        loads.append(copy)

    lane = lax.broadcasted_iota(jnp.int32, (8, 128), 1)
    row = lax.broadcasted_iota(jnp.int32, (8, 128), 0)
    row0, row7, lane0, lane127 = row == 0, row == 7, lane == 0, lane == 127
    quarter = jnp.bitwise_and(lane, 3)
    x_in = ((row < 4) & has_right) | ((row >= 4) & has_left)
    y_in = ((lane < 64) & (iy < ny - 1)) | ((lane >= 64) & (iy > 0))
    inside = {OWN: None, XH: x_in, YH: y_in, XYH: x_in & y_in}
    flipped = iz == 1
    hz = jnp.where(flipped, -HALF, HALF)

    def plane(z):
        return jnp.where(flipped, 7 - z, z)

    def put(f, z, t, value):
        ext[(f * 10 + z) * 4 + t] = value

    def get(f, z, t):
        return ext[(f * 10 + z) * 4 + t]

    for i in range(3):
        loads[i].wait()
    group = iy * nz + iz
    per_row = 128 // FAC_DEV
    stride = (ny * nz) // per_row
    row_of = [lax.rem(ix + o + nx, nx) * stride + group // per_row for o in (0, 1, -1)]
    ids = jnp.broadcast_to(jnp.concatenate([tab[...], tab[...]], axis=1), (8, 128))
    id_row = lax.shift_right_logical(ids, 7)
    id_lane = jnp.bitwise_and(ids, 127)
    lut = jnp.zeros((8, 128), F32)
    for o in range(3):
        line = jnp.broadcast_to(imp[pl.ds(row_of[o], 1), :], (8, 128))
        lut = jnp.where(id_row == row_of[o], jnp.take_along_axis(line, id_lane, axis=1), lut)
    lut = lut * FULL
    place = jnp.where(id_row == row_of[0], 0, jnp.where(id_row == row_of[1], 32, 64)) + jnp.bitwise_and(ids, 31)
    for z in range(8):
        names = slo[plane(z)]
        value = jnp.take_along_axis(lut, jnp.maximum(names - 1, 0), axis=1)
        put(DAMP, z, OWN, jnp.where(names > 0, value, 0.0))
    for i in range(3, 6):
        loads[i].wait()

    def fluxes(s, w):
        fz = [w[0] * v for v in s]
        fx = [w[1] * v for v in s]
        fy = [w[2] * v for v in s]
        fz[0], fz[1] = fz[0] + s[1], fz[1] + s[0]
        fx[0], fx[2] = fx[0] + s[2], fx[2] + s[0]
        fy[0], fy[3] = fy[0] + s[3], fy[3] + s[0]
        return fz, fx, fy

    zero = jnp.zeros((8, 128), F32)
    y_high, y_low = [zero] * 4, [zero] * 4
    for z in reversed(range(8)):
        zi = plane(z)
        own = [mid[c, zi] for c in range(4)] + [upp[c, zi] for c in range(4)] + [win[c, zi] for c in range(3)]
        own.append(get(DAMP, z, OWN))
        for f in range(FIELDS):
            value = own[f]
            if f < DAMP:
                put(f, z, OWN, value)
            if z >= 6:
                zbuf[(7 - z) * FIELDS + f] = value
            n = (7 - z) * FIELDS + f
            k = n % 4
            if k == 0:
                x_high = x_low = zero
            moved = pltpu.roll(value, (2 * k + 2) % 8, 0)
            pair, k_next = row // 2, (k + 1) % 4
            x_high = jnp.where(pair == k, moved, x_high)
            x_low = jnp.where(pair == k_next, moved, x_low)
            if k == 3:
                xbuf[0, n // 4] = x_high
                xbuf[1, n // 4] = x_low
            t, k = n // 32, n % 32
            moved = pltpu.roll(value, (4 * k + 2) % 128, 1)
            quad = lane // 4 == k
            y_high[t] = jnp.where(quad & (quarter < 2), moved, y_high[t])
            y_low[t] = jnp.where(quad & (quarter >= 2), moved, y_low[t])
        fz, fx, fy = fluxes(own[:4], own[8:11])
        for c in range(4):
            if z == 5:
                zbuf[2 * FIELDS + c] = fz[c]
            xbuf[0, 24 + c, pl.ds(z, 1), :] = fx[c][5:6]
            xbuf[1, 24 + c, pl.ds(z, 1), :] = fx[c][2:3]
            k = c * 8 + z
            moved = pltpu.roll(fy[c], (4 * k + 3) % 128, 1)
            y_high[3] = jnp.where(lane == 4 * k, moved, y_high[3])
            y_low[3] = jnp.where(lane == (4 * k + 5) % 128, moved, y_low[3])
    for t in range(4):
        ybuf[0, t] = y_high[t]
        ybuf[1, t] = y_low[t]

    halo = []

    def post(src, dst, to, dx=0):
        i = len(halo)
        send_if, recv_if = {0: (None, None), 1: (has_right, has_left), -1: (has_left, has_right)}[dx]
        halo.append(Sent(src, dst, ss.at[i], rs.at[i], to, send_if, recv_if))

    post(zbuf, zr, device(0, 0, 1))
    for side, d in ((0, 1), (1, -1)):
        post(xbuf.at[side], xr.at[side], device(d, 0, 0), d)
        post(xbuf.at[side, pl.ds(0, 6)], xzr.at[side], device(d, 0, 1), d)
        post(ybuf.at[side], yr.at[side], device(0, d, 0))
        post(ybuf.at[side, 0], yzr.at[side], device(0, d, 1))
        for x_side, e in ((0, 1), (1, -1)):
            post(ybuf.at[side, pl.ds(0, 3)], xyr.at[x_side, side], device(e, d, 0), e)
            post(ybuf.at[side, 0], xyzr.at[x_side, side], device(e, d, 1), e)

    @pl.when(has_left & has_right)
    def _():
        pl.semaphore_wait(barrier, 17)

    @pl.when(ix == 0)
    def _():
        pl.semaphore_wait(barrier, 11)
        pl.semaphore_signal(barrier, inc=1, device_id=(nx - 1, iy, iz), device_id_type=MESH)

    @pl.when(ix == nx - 1)
    def _():
        pl.semaphore_wait(barrier, 12)
        pl.semaphore_signal(barrier, inc=1, device_id=(0, iy, iz), device_id_type=MESH)

    for sent in halo:
        sent.start()

    def add_products(k, base):
        for z in range(8):
            zi = plane(z)
            total = get(base, z, OWN) * sav[k, 0, zi]
            for c in range(1, 4):
                total = total + get(base + c, z, OWN) * sav[k, c, zi]
            prod[z] = total if k == 0 else prod[z] + total

    loads[6].wait()
    add_products(0, 0)
    for sent in halo:
        sent.wait_recv()

    def masked(f, t, value):
        if f < 4 or WIND <= f < DAMP:
            return jnp.where(inside[t], value, 0.0)
        return value

    def both_y(high, low):
        return jnp.where(quarter < 2, high, low)

    y_own = [both_y(yr[0, t], yr[1, t]) for t in range(3)]
    y_top = both_y(yzr[0], yzr[1])
    xy_own = [jnp.where(row < 4, both_y(xyr[1, 0, t], xyr[1, 1, t]), both_y(xyr[0, 0, t], xyr[0, 1, t])) for t in range(3)]
    xy_top = jnp.where(row < 4, both_y(xyzr[1, 0], xyzr[1, 1]), both_y(xyzr[0, 0], xyzr[0, 1]))
    for z in range(10):
        for f in range(FIELDS):
            top = z >= 8
            light = f < 4 or WIND <= f < DAMP
            n = ((z - 8) if top else (7 - z)) * FIELDS + f
            if top:
                put(f, z, OWN, zr[n])
            if z == 9 and not light:
                continue
            src = xzr if top else xr
            k = n % 4
            value = jnp.where(row // 2 == k, src[0, n // 4], src[1, n // 4])
            put(f, z, XH, masked(f, XH, pltpu.roll(value, (6 - 2 * k) % 8, 0)))
            t, k = n // 32, n % 32
            shift = (126 - 4 * k) % 128
            put(f, z, YH, masked(f, YH, pltpu.roll(y_top if top else y_own[t], shift, 1)))
            if z < 8 or (z == 8 and light):
                put(f, z, XYH, masked(f, XYH, pltpu.roll(xy_top if top else xy_own[t], shift, 1)))

    def across(own, far, r_up, r_dn, axis):
        size = own.shape[axis]
        up, dn = size - 1, 1
        own_up, own_dn = pltpu.roll(own, up, axis), pltpu.roll(own, dn, axis)
        far_up, far_dn = pltpu.roll(far, up, axis), pltpu.roll(far, dn, axis)
        return (
            jnp.where(r_up, far_up, own_up) - jnp.where(r_dn, far_dn, own_dn),
            jnp.where(r_up, own_up, far_up) - jnp.where(r_dn, own_dn, far_dn),
        )

    y_flux = jnp.where(quarter == 0, yr[0, 3], yr[1, 3])
    y_third = (lane == 125) | (lane == 2)

    def flux_plane(src, z, tiles, first):
        result = {}
        for t in tiles:
            fz, fx, fy = fluxes([get(src + c, z, t) for c in range(4)], [get(WIND + c, z, t) for c in range(3)])
            if first and z < 8 and t == XH:
                for c in range(4):
                    lo = xr[0, 24 + c, pl.ds(z, 1), :]
                    hi = xr[1, 24 + c, pl.ds(z, 1), :]
                    fx[c] = jnp.where(row == 5, lo, jnp.where(row == 2, hi, fx[c]))
            if first and z < 8 and t == YH:
                for c in range(4):
                    k = c * 8 + z
                    fy[c] = jnp.where(y_third, pltpu.roll(y_flux, (125 - 4 * k) % 128, 1), fy[c])
            result[t] = (fz, fx, fy)
        return result

    def step(src, dst, flux_tiles, new_tiles, top_flux=None, keep=None):
        count = len(flux_tiles)
        first = top_flux is not None
        before, here = None, flux_plane(src, 0, flux_tiles[0], first)
        for z in range(len(new_tiles)):
            after = flux_plane(src, z + 1, flux_tiles[z + 1], first) if z + 1 < count else None
            for c in range(4):
                f = {t: here[t] for t in flux_tiles[z]}
                dx, dy = {}, {}
                dx[OWN], dx[XH] = across(f[OWN][1][c], f[XH][1][c], row7, row0, 0)
                dy[OWN], dy[YH] = across(f[OWN][2][c], f[YH][2][c], lane127, lane0, 1)
                if XYH in f:
                    dx[YH], dx[XYH] = across(f[YH][1][c], f[XYH][1][c], row7, row0, 0)
                    dy[XH], dy[XYH] = across(f[XH][2][c], f[XYH][2][c], lane127, lane0, 1)
                for t in new_tiles[z]:
                    up = after[t][0][c] if after is not None else top_flux[c]
                    dz = up if before is None else up - before[t][0][c]
                    value = get(dst + c, z, t) + HALF * (dx[t] + dy[t]) + hz * dz - get(DAMP, z, t) * get(src + c, z, t)
                    if t != OWN:
                        value = jnp.where(inside[t], value, 0.0)
                    put(dst + c, z, t, value)
                    if keep is not None:
                        keep(c, z, value)
            before, here = here, after

    every = [OWN, XH, YH, XYH]
    sides = [OWN, XH, YH]
    step(0, 4, [every] * 9 + [sides], [every] * 8 + [sides, [OWN]], [zr[2 * FIELDS + c] for c in range(4)])
    add_products(1, 4)
    step(4, 0, [every] * 8 + [sides, [OWN]], [sides] * 8 + [[OWN]])
    add_products(2, 0)
    third = [[None] * 8 for _ in range(4)]

    def keep(c, z, value):
        third[c][z] = value
        out[0, c, plane(z)] = value

    step(0, 4, [sides] * 8 + [[OWN]], [[OWN]] * 8, None, keep)

    low, high = zero, zero
    allf = []
    for z in range(8):
        fz, fx, fy = fluxes([third[c][z] for c in range(4)], [get(WIND + c, z, OWN) for c in range(3)])
        allf.append((fz, fx, fy))
        for c in range(4):
            n = c * 8 + z
            xs[0, pl.ds(n, 1), :] = fx[c][7:8]
            xs[1, pl.ds(n, 1), :] = fx[c][0:1]
            p = 2 * n + 1
            moved = pltpu.roll(fy[c], (p + 1) % 128, 1)
            high = jnp.where(lane == p, moved, high)
            low = jnp.where(lane == (p + 1) % 128, moved, low)
    ys[0], ys[1] = high, low
    for c in range(4):
        zs[c] = allf[7][0][c]
    faces = [
        Sent(ys.at[0], yf.at[0], fs.at[0], fr.at[0], device(0, 1, 0)),
        Sent(ys.at[1], yf.at[1], fs.at[1], fr.at[1], device(0, -1, 0)),
        Sent(zs, zf, fs.at[2], fr.at[2], device(0, 0, 1)),
        Sent(xs.at[0], xf.at[0], fs.at[3], fr.at[3], device(1, 0, 0), has_right, has_left),
        Sent(xs.at[1], xf.at[1], fs.at[4], fr.at[4], device(-1, 0, 0), has_left, has_right),
    ]
    for sent in faces:
        sent.start()
    add_products(3, 4)

    for s in range(64):
        total = zero
        for z in range(8):
            total = total + jnp.where(slo[plane(z)] == s + 1, prod[z], 0.0)
        smat[pl.ds(s, 1), :] = jnp.sum(total, axis=0, keepdims=True)
    sums = jnp.sum(smat[...], axis=1, keepdims=True) * (-FULL)
    turned = jnp.transpose(jnp.broadcast_to(place[0:1], (128, 128)))[0:64]
    wide = lax.broadcasted_iota(jnp.int32, (64, 128), 1)
    facades = jnp.sum(jnp.where(turned == wide, sums, 0.0), axis=0, keepdims=True)
    gs[...] = jnp.broadcast_to(facades, (8, 128))

    @pl.when(ix == 0)
    def _():
        pl.semaphore_wait(barrier, 1)

    parts = [
        Sent(gs, gr.at[0], g_ss.at[0], g_rs.at[0], device(1, 0, 0)),
        Sent(gs, gr.at[1], g_ss.at[1], g_rs.at[1], device(-1, 0, 0)),
    ]
    for sent in parts:
        sent.start()

    for z in range(8):
        d = get(DAMP, z, OWN)
        for c in range(4):
            fz, fx, fy = (allf[z][i][c] for i in range(3))
            dx = jnp.where(row7, 0.0, pltpu.roll(fx, 7, 0)) - jnp.where(row0, 0.0, pltpu.roll(fx, 1, 0))
            dy = jnp.where(lane127, 0.0, pltpu.roll(fy, 127, 1)) - jnp.where(lane0, 0.0, pltpu.roll(fy, 1, 1))
            value = get(c, z, OWN) + HALF * (dx + dy) - d * third[c][z]
            if z < 7:
                value = value + hz * allf[z + 1][0][c]
            if z > 0:
                value = value - hz * allf[z - 1][0][c]
            part[c * 8 + z] = value

    for sent in faces:
        sent.wait_recv()
    south = jnp.where(iy > 0, -yf[0], 0.0)
    north = jnp.where(iy < ny - 1, pltpu.roll(yf[1], 126, 1), 0.0)
    rim = HALF * jnp.where(jnp.bitwise_and(lane, 1) == 1, south, north)
    at_left, at_right = row0 & has_left, row7 & has_right
    for z in range(8):
        for c in range(4):
            n = c * 8 + z
            value = part[n]
            edge = pltpu.roll(rim, 128 - (2 * n + 1), 1)
            value = value + jnp.where(lane0 | lane127, edge, 0.0)
            lrow = xf[0, pl.ds(n, 1), :] * (-HALF)
            rrow = xf[1, pl.ds(n, 1), :] * HALF
            value = value + jnp.where(at_left, lrow, jnp.where(at_right, rrow, 0.0))
            if z == 7:
                value = value + hz * zf[c]
            out[1, c, plane(z)] = value
    for sent in parts:
        sent.wait_recv()
    total = gs[...] + pltpu.roll(gr[0], 96, 1) + pltpu.roll(gr[1], 64, 1)
    grad[...] = total[0, 0:FAC_DEV]
    for sent in halo + faces + parts:
        sent.wait_send()


def local(sizes, adjoint, saved_state, wind_field, facade_slot, facade_table, impedance):
    imp = impedance.reshape(-1, 128)
    hbm_spec = pl.BlockSpec(memory_space=pltpu.HBM)
    vmem_spec = pl.BlockSpec(memory_space=pltpu.VMEM)
    v = pltpu.VMEM
    dma = pltpu.SemaphoreType.DMA
    steps = saved_state.shape[0]
    assert steps == 4
    out, grad = pl.pallas_call(
        functools.partial(kernel, sizes),
        out_shape=[
            jax.ShapeDtypeStruct(adjoint.shape, F32),
            jax.ShapeDtypeStruct((FAC_DEV,), F32),
        ],
        in_specs=[hbm_spec] * 6,
        out_specs=[vmem_spec, vmem_spec],
        scratch_shapes=[
            v((4, 8, 8, 128), F32),
            v((4, 8, 8, 128), F32),
            v((steps, 4, 8, 8, 128), F32),
            v((3, 8, 8, 128), F32),
            v((8, 8, 128), jnp.int32),
            v((1, 64), jnp.int32),
            v((128, 128), F32),
            v((FIELDS * 10 * 4, 8, 128), F32),
            v((32, 8, 128), F32),
            v((8, 8, 128), F32),
            v((2, 28, 8, 128), F32),
            v((2, 4, 8, 128), F32),
            v((28, 8, 128), F32),
            v((2, 28, 8, 128), F32),
            v((2, 6, 8, 128), F32),
            v((2, 4, 8, 128), F32),
            v((2, 8, 128), F32),
            v((28, 8, 128), F32),
            v((2, 2, 3, 8, 128), F32),
            v((2, 2, 8, 128), F32),
            v((2, 32, 128), F32),
            v((2, 8, 128), F32),
            v((4, 8, 128), F32),
            v((2, 32, 128), F32),
            v((2, 8, 128), F32),
            v((4, 8, 128), F32),
            v((64, 128), F32),
            v((8, 128), F32),
            v((2, 8, 128), F32),
            dma((7,)), dma((17,)), dma((17,)), dma((5,)), dma((5,)), dma((2,)), dma((2,)),
        ],
        compiler_params=pltpu.CompilerParams(
            collective_id=0, has_side_effects=True, vmem_limit_bytes=32 << 20
        ),
    )(*[pltpu.with_memory_space_constraint(a, pltpu.HBM)
        for a in (adjoint, saved_state, wind_field, facade_slot, facade_table, imp)])
    return out, grad


def solution(mesh):
    sizes = tuple(mesh.shape[a] for a in ("gx", "gy", "gz"))
    return jax.shard_map(
        functools.partial(local, sizes),
        mesh=mesh,
        in_specs=(
            P(None, None, "gz", "gx", "gy"),
            P(None, None, "gz", "gx", "gy"),
            P(None, "gz", "gx", "gy"),
            P("gz", "gx", "gy"),
            P("gz", "gx", "gy", None),
            P(),
        ),
        out_specs=(P(None, None, "gz", "gx", "gy"), P(("gx", "gy", "gz"))),
        check_vma=False,
    )
```

time: 166 us -> 26.7 us (0.16)
  the two profiles are of different devices: /device:TPU:128 before, /device:TPU:2 now
where the time goes in v3:
time: 26.7 us; the launch traced here: 26.5 us
  Pallas kernels  24.7 us (93%)
  local copies, waits for them, and re-layouts  1.22 us (5%)
  between operations  0.64 us (2%)
    pallas_call x1, Pallas kernels, local(): pl.pallas_call(functools.partial(kernel, sizes), out_shape=[jax.ShapeDtyp...  24.7 us
    unnamed x2, local copies, waits for them, and re-layouts  1.22 us

profile of v3, /device:TPU:2, one launch (start us, length us, event | category | flops | bytes accessed | tf_op | source)
XLA Modules:
  0.0 26.5 jit_solution(12625786620668285895)
XLA Ops:
  0.6 24.7 %shard_map.77 = (f32[2,4,8,8,128]{4,3,2,1,0:T(8,128)S(1)}, f32[32]{0:T(128)S(1)}) custom-call(f32[2,4,8,8,128]{4,3,2,1,0:T(8,128)} %adj.1, f32[4,4,8,8,128]{4,3,2,1,0:T(8,128)} %saved.1, f32[3,8,8,128]{3,2,1,0:T(8,128)} %wind.1, s32[8,8,128]{2,1,0:T(8,128)} %slot.1, s32[1,1,1,64]{3,2,1,0:T(1,128)} %table.1, f32[128,128]{1,0:T(8,128)} %bitcast.1), custom_call_target="tpu_custom_call" | custom-call | tf_op jit(solution)/shard_map/pallas_call | solution.py:413
  25.3 0.7 %copy.10 = f32[2,4,8,8,128]{4,3,2,1,0:T(8,128)} copy(f32[2,4,8,8,128]{4,3,2,1,0:T(8,128)S(1)} %get-tuple-element.4) | data formatting | bytes 524288
  26.0 0.5 %copy.11 = f32[32]{0:T(128)} copy(f32[32]{0:T(128)S(1)} %get-tuple-element.5) | data formatting | bytes 256

commit v4 on v3

--- a/solution.py
+++ b/solution.py
@@ -44,7 +44,7 @@
 
 def kernel(sizes, adj, saved, wind, slot, table, impedance, out, grad,
            mid, upp, sav, win, slo, tab, imp, ext, part, prod,
-           xbuf, ybuf, zbuf, xr, xzr, yr, yzr, zr, xyr, xyzr,
+           xbuf, xzbuf, ybuf, xybuf, zbuf, xr, xzr, yr, yzr, zr, xyr, xyzr,
            xs, ys, zs, xf, yf, zf, smat, gs, gr,
            in_sem, ss, rs, fs, fr, g_ss, g_rs):
     nx, ny, nz = sizes
@@ -127,17 +127,45 @@
         return fz, fx, fy
 
     zero = jnp.zeros((8, 128), F32)
-    y_high, y_low = [zero] * 4, [zero] * 4
+
+    def within(level, allf, upper, store):
+        for z in range(8):
+            d = get(DAMP, z, OWN)
+            for c in range(4):
+                fz, fx, fy = (allf[z][i][c] for i in range(3))
+                dx = jnp.where(row7, 0.0, pltpu.roll(fx, 7, 0)) - jnp.where(row0, 0.0, pltpu.roll(fx, 1, 0))
+                dy = jnp.where(lane127, 0.0, pltpu.roll(fy, 127, 1)) - jnp.where(lane0, 0.0, pltpu.roll(fy, 1, 1))
+                value = upper(c, z) + HALF * (dx + dy) - d * level(c, z)
+                if 0 < z < 7:
+                    value = value + hz * (allf[z + 1][0][c] - allf[z - 1][0][c])
+                elif z == 0:
+                    value = value + hz * allf[1][0][c]
+                else:
+                    value = value - hz * allf[6][0][c]
+                store(c, z, value)
+
+    allf = []
+    for z in range(8):
+        zi = plane(z)
+        own = [mid[c, zi] for c in range(4)]
+        wz = [win[c, zi] for c in range(3)]
+        for c in range(4):
+            put(c, z, OWN, own[c])
+        for c in range(3):
+            put(WIND + c, z, OWN, wz[c])
+        allf.append(fluxes(own, wz))
+    within(
+        lambda c, z: get(c, z, OWN), allf, lambda c, z: upp[c, plane(z)], lambda c, z, value: put(4 + c, z, OWN, value)
+    )
+
+    y_high, y_low = [zero] * 3, [zero] * 3
     for z in reversed(range(8)):
-        zi = plane(z)
-        own = [mid[c, zi] for c in range(4)] + [upp[c, zi] for c in range(4)] + [win[c, zi] for c in range(3)]
-        own.append(get(DAMP, z, OWN))
         for f in range(FIELDS):
-            value = own[f]
-            if f < DAMP:
-                put(f, z, OWN, value)
-            if z >= 6:
-                zbuf[(7 - z) * FIELDS + f] = value
+            value = get(f, z, OWN)
+            if z == 7:
+                zbuf[f] = value
+            if z == 6 and 4 <= f <= WIND:
+                zbuf[FIELDS + f - 4] = value
             n = (7 - z) * FIELDS + f
             k = n % 4
             if k == 0:
@@ -154,19 +182,23 @@
             quad = lane // 4 == k
             y_high[t] = jnp.where(quad & (quarter < 2), moved, y_high[t])
             y_low[t] = jnp.where(quad & (quarter >= 2), moved, y_low[t])
-        fz, fx, fy = fluxes(own[:4], own[8:11])
-        for c in range(4):
-            if z == 5:
-                zbuf[2 * FIELDS + c] = fz[c]
-            xbuf[0, 24 + c, pl.ds(z, 1), :] = fx[c][5:6]
-            xbuf[1, 24 + c, pl.ds(z, 1), :] = fx[c][2:3]
-            k = c * 8 + z
-            moved = pltpu.roll(fy[c], (4 * k + 3) % 128, 1)
-            y_high[3] = jnp.where(lane == 4 * k, moved, y_high[3])
-            y_low[3] = jnp.where(lane == (4 * k + 5) % 128, moved, y_low[3])
-    for t in range(4):
-        ybuf[0, t] = y_high[t]
-        ybuf[1, t] = y_low[t]
+            if z == 7 and f < WIND + 2:
+                xzbuf[0, pl.ds(f, 1), :] = value[7:8]
+                xzbuf[1, pl.ds(f, 1), :] = value[0:1]
+    for c in range(4):
+        xzbuf[0, pl.ds(10 + c, 1), :] = allf[7][0][c][6:7]
+        xzbuf[1, pl.ds(10 + c, 1), :] = allf[7][0][c][1:2]
+        xzbuf[0, pl.ds(14 + c, 1), :] = allf[6][1][c][7:8]
+        xzbuf[1, pl.ds(14 + c, 1), :] = allf[6][1][c][0:1]
+    for side, tiles in ((0, y_high), (1, y_low)):
+        xy_high, xy_low = zero, zero
+        for t in range(3):
+            ybuf[side, t] = tiles[t]
+            moved = pltpu.roll(tiles[t], (2 * t + 2) % 8, 0)
+            xy_high = jnp.where(row // 2 == t, moved, xy_high)
+            xy_low = jnp.where(row // 2 == t + 1, moved, xy_low)
+        xybuf[0, side] = xy_high
+        xybuf[1, side] = xy_low
 
     halo = []
 
@@ -178,12 +210,12 @@
     post(zbuf, zr, device(0, 0, 1))
     for side, d in ((0, 1), (1, -1)):
         post(xbuf.at[side], xr.at[side], device(d, 0, 0), d)
-        post(xbuf.at[side, pl.ds(0, 6)], xzr.at[side], device(d, 0, 1), d)
+        post(xzbuf.at[side], xzr.at[side], device(d, 0, 1), d)
         post(ybuf.at[side], yr.at[side], device(0, d, 0))
         post(ybuf.at[side, 0], yzr.at[side], device(0, d, 1))
         for x_side, e in ((0, 1), (1, -1)):
-            post(ybuf.at[side, pl.ds(0, 3)], xyr.at[x_side, side], device(e, d, 0), e)
-            post(ybuf.at[side, 0], xyzr.at[x_side, side], device(e, d, 1), e)
+            post(xybuf.at[x_side, side], xyr.at[x_side, side], device(e, d, 0), e)
+            post(xybuf.at[x_side, side], xyzr.at[x_side, side], device(e, d, 1), e)
 
     @pl.when(has_left & has_right)
     def _():
@@ -225,26 +257,37 @@
 
     y_own = [both_y(yr[0, t], yr[1, t]) for t in range(3)]
     y_top = both_y(yzr[0], yzr[1])
-    xy_own = [jnp.where(row < 4, both_y(xyr[1, 0, t], xyr[1, 1, t]), both_y(xyr[0, 0, t], xyr[0, 1, t])) for t in range(3)]
-    xy_top = jnp.where(row < 4, both_y(xyzr[1, 0], xyzr[1, 1]), both_y(xyzr[0, 0], xyzr[0, 1]))
-    for z in range(10):
+
+    def xy_tile(src, t):
+        value = jnp.where(row // 2 == t, both_y(src[0, 0], src[0, 1]), both_y(src[1, 0], src[1, 1]))
+        return pltpu.roll(value, (6 - 2 * t) % 8, 0)
+
+    xy_own = [xy_tile(xyr, t) for t in range(3)]
+    xy_top = xy_tile(xyzr, 0)
+    for z in range(8):
         for f in range(FIELDS):
-            top = z >= 8
-            light = f < 4 or WIND <= f < DAMP
-            n = ((z - 8) if top else (7 - z)) * FIELDS + f
-            if top:
-                put(f, z, OWN, zr[n])
-            if z == 9 and not light:
-                continue
-            src = xzr if top else xr
+            n = (7 - z) * FIELDS + f
             k = n % 4
-            value = jnp.where(row // 2 == k, src[0, n // 4], src[1, n // 4])
+            value = jnp.where(row // 2 == k, xr[0, n // 4], xr[1, n // 4])
             put(f, z, XH, masked(f, XH, pltpu.roll(value, (6 - 2 * k) % 8, 0)))
             t, k = n // 32, n % 32
             shift = (126 - 4 * k) % 128
-            put(f, z, YH, masked(f, YH, pltpu.roll(y_top if top else y_own[t], shift, 1)))
-            if z < 8 or (z == 8 and light):
-                put(f, z, XYH, masked(f, XYH, pltpu.roll(xy_top if top else xy_own[t], shift, 1)))
+            put(f, z, YH, masked(f, YH, pltpu.roll(y_own[t], shift, 1)))
+            if f < DAMP:
+                put(f, z, XYH, masked(f, XYH, pltpu.roll(xy_own[t], shift, 1)))
+    for f in range(FIELDS):
+        put(f, 8, OWN, zr[f])
+        if 4 <= f <= WIND:
+            put(f, 9, OWN, zr[FIELDS + f - 4])
+        if f < WIND + 2:
+            value = jnp.where(row == 7, xzr[0, pl.ds(f, 1), :], xzr[1, pl.ds(f, 1), :])
+            put(f, 8, XH, masked(f, XH, value))
+        shift = (126 - 4 * f) % 128
+        if f < DAMP:
+            put(f, 8, YH, masked(f, YH, pltpu.roll(y_top, shift, 1)))
+        if f < 4 or WIND <= f < DAMP:
+            put(f, 8, XYH, masked(f, XYH, pltpu.roll(xy_top, shift, 1)))
+            put(f, 9, YH, masked(f, YH, pltpu.roll(y_top, (126 - 4 * (FIELDS + f)) % 128, 1)))
 
     def across(own, far, r_up, r_dn, axis):
         size = own.shape[axis]
@@ -256,31 +299,54 @@
             jnp.where(r_up, own_up, far_up) - jnp.where(r_dn, own_dn, far_dn),
         )
 
-    y_flux = jnp.where(quarter == 0, yr[0, 3], yr[1, 3])
-    y_third = (lane == 125) | (lane == 2)
-
-    def flux_plane(src, z, tiles, first):
-        result = {}
-        for t in tiles:
-            fz, fx, fy = fluxes([get(src + c, z, t) for c in range(4)], [get(WIND + c, z, t) for c in range(3)])
-            if first and z < 8 and t == XH:
+    def flux_tile(src, z, t):
+        return fluxes([get(src + c, z, t) for c in range(4)], [get(WIND + c, z, t) for c in range(3)])
+
+    def flux_plane(src, z, tiles):
+        return {t: flux_tile(src, z, t) for t in tiles}
+
+    def seam(flux, r_up, r_dn, axis):
+        size = flux.shape[axis]
+        return jnp.where(r_up, pltpu.roll(flux, size - 1, axis), 0.0) - jnp.where(r_dn, pltpu.roll(flux, 1, axis), 0.0)
+
+    def first_step():
+        beside_x = {OWN: XH, XH: OWN, YH: XYH, XYH: YH}
+        beside_y = {OWN: YH, YH: OWN, XH: XYH, XYH: XH}
+        here = None
+        after = flux_plane(0, 0, [OWN, XH, YH, XYH])
+        for z in range(10):
+            before, here = here, after
+            after = None
+            if z + 1 < 9:
+                after = flux_plane(0, z + 1, [OWN, XH, YH, XYH])
+                if z + 1 == 8:
+                    fz = after[XH][0]
+                    for c in range(4):
+                        lo, hi = xzr[0, pl.ds(10 + c, 1), :], xzr[1, pl.ds(10 + c, 1), :]
+                        fz[c] = jnp.where(row == 6, lo, jnp.where(row == 1, hi, fz[c]))
+            elif z + 1 == 9:
+                fx = []
                 for c in range(4):
-                    lo = xr[0, 24 + c, pl.ds(z, 1), :]
-                    hi = xr[1, 24 + c, pl.ds(z, 1), :]
-                    fx[c] = jnp.where(row == 5, lo, jnp.where(row == 2, hi, fx[c]))
-            if first and z < 8 and t == YH:
+                    lo, hi = xzr[0, pl.ds(14 + c, 1), :], xzr[1, pl.ds(14 + c, 1), :]
+                    fx.append(jnp.where(inside[XH], jnp.where(row == 7, lo, hi), 0.0))
+                after = {XH: (None, fx, None), YH: flux_tile(0, 9, YH)}
+            for t in [OWN, XH, YH, XYH] if z < 8 else [OWN, XH, YH] if z == 8 else [OWN]:
                 for c in range(4):
-                    k = c * 8 + z
-                    fy[c] = jnp.where(y_third, pltpu.roll(y_flux, (125 - 4 * k) % 128, 1), fy[c])
-            result[t] = (fz, fx, fy)
-        return result
-
-    def step(src, dst, flux_tiles, new_tiles, top_flux=None, keep=None):
-        count = len(flux_tiles)
-        first = top_flux is not None
-        before, here = None, flux_plane(src, 0, flux_tiles[0], first)
+                    sx = seam(here[beside_x[t]][1][c], row7, row0, 0)
+                    sy = seam(here[beside_y[t]][2][c], lane127, lane0, 1)
+                    value = get(4 + c, z, t) + HALF * (sx + sy)
+                    if z == 7:
+                        value = value + hz * after[t][0][c]
+                    if z == 8:
+                        value = value - hz * before[t][0][c]
+                    if t != OWN:
+                        value = jnp.where(inside[t], value, 0.0)
+                    put(4 + c, z, t, value)
+
+    def step(src, dst, flux_tiles, new_tiles, keep=None):
+        before, here = None, flux_plane(src, 0, flux_tiles[0])
         for z in range(len(new_tiles)):
-            after = flux_plane(src, z + 1, flux_tiles[z + 1], first) if z + 1 < count else None
+            after = flux_plane(src, z + 1, flux_tiles[z + 1])
             for c in range(4):
                 f = {t: here[t] for t in flux_tiles[z]}
                 dx, dy = {}, {}
@@ -290,7 +356,7 @@
                     dx[YH], dx[XYH] = across(f[YH][1][c], f[XYH][1][c], row7, row0, 0)
                     dy[XH], dy[XYH] = across(f[XH][2][c], f[XYH][2][c], lane127, lane0, 1)
                 for t in new_tiles[z]:
-                    up = after[t][0][c] if after is not None else top_flux[c]
+                    up = after[t][0][c]
                     dz = up if before is None else up - before[t][0][c]
                     value = get(dst + c, z, t) + HALF * (dx[t] + dy[t]) + hz * dz - get(DAMP, z, t) * get(src + c, z, t)
                     if t != OWN:
@@ -302,7 +368,7 @@
 
     every = [OWN, XH, YH, XYH]
     sides = [OWN, XH, YH]
-    step(0, 4, [every] * 9 + [sides], [every] * 8 + [sides, [OWN]], [zr[2 * FIELDS + c] for c in range(4)])
+    first_step()
     add_products(1, 4)
     step(4, 0, [every] * 8 + [sides, [OWN]], [sides] * 8 + [[OWN]])
     add_products(2, 0)
@@ -312,7 +378,7 @@
         third[c][z] = value
         out[0, c, plane(z)] = value
 
-    step(0, 4, [sides] * 8 + [[OWN]], [[OWN]] * 8, None, keep)
+    step(0, 4, [sides] * 8 + [[OWN]], [[OWN]] * 8, keep)
 
     low, high = zero, zero
     allf = []
@@ -363,18 +429,10 @@
     for sent in parts:
         sent.start()
 
-    for z in range(8):
-        d = get(DAMP, z, OWN)
-        for c in range(4):
-            fz, fx, fy = (allf[z][i][c] for i in range(3))
-            dx = jnp.where(row7, 0.0, pltpu.roll(fx, 7, 0)) - jnp.where(row0, 0.0, pltpu.roll(fx, 1, 0))
-            dy = jnp.where(lane127, 0.0, pltpu.roll(fy, 127, 1)) - jnp.where(lane0, 0.0, pltpu.roll(fy, 1, 1))
-            value = get(c, z, OWN) + HALF * (dx + dy) - d * third[c][z]
-            if z < 7:
-                value = value + hz * allf[z + 1][0][c]
-            if z > 0:
-                value = value - hz * allf[z - 1][0][c]
-            part[c * 8 + z] = value
+    def hold(c, z, value):
+        part[c * 8 + z] = value
+
+    within(lambda c, z: third[c][z], allf, lambda c, z: get(c, z, OWN), hold)
 
     for sent in faces:
         sent.wait_recv()
@@ -429,15 +487,17 @@
             v((FIELDS * 10 * 4, 8, 128), F32),
             v((32, 8, 128), F32),
             v((8, 8, 128), F32),
-            v((2, 28, 8, 128), F32),
-            v((2, 4, 8, 128), F32),
-            v((28, 8, 128), F32),
-            v((2, 28, 8, 128), F32),
-            v((2, 6, 8, 128), F32),
-            v((2, 4, 8, 128), F32),
+            v((2, 24, 8, 128), F32),
+            v((2, 24, 128), F32),
+            v((2, 3, 8, 128), F32),
+            v((2, 2, 8, 128), F32),
+            v((17, 8, 128), F32),
+            v((2, 24, 8, 128), F32),
+            v((2, 24, 128), F32),
+            v((2, 3, 8, 128), F32),
             v((2, 8, 128), F32),
-            v((28, 8, 128), F32),
-            v((2, 2, 3, 8, 128), F32),
+            v((17, 8, 128), F32),
+            v((2, 2, 8, 128), F32),
             v((2, 2, 8, 128), F32),
             v((2, 32, 128), F32),
             v((2, 8, 128), F32),

time: 26.7 us -> 24.6 us (0.921)
  Pallas kernels: 24.7 us -> 22.6 us
    pallas_call x1, Pallas kernels: 24.7 us -> 22.6 us  [local(): pl.pallas_call(functools.partial(kernel, sizes), out_shape=[jax.ShapeDtyp...]
where the time goes in v4:
time: 24.6 us; the launch traced here: 24.5 us
  Pallas kernels  22.6 us (92%)
  local copies, waits for them, and re-layouts  1.22 us (5%)
  between operations  0.64 us (3%)
    pallas_call x1, Pallas kernels, local(): pl.pallas_call(functools.partial(kernel, sizes), out_shape=[jax.ShapeDtyp...  22.6 us
    unnamed x2, local copies, waits for them, and re-layouts  1.22 us

profile of v4, /device:TPU:2, one launch (start us, length us, event | category | flops | bytes accessed | tf_op | source)
XLA Modules:
  0.0 24.5 jit_solution(11194944473921636295)
XLA Ops:
  0.6 22.6 %shard_map.77 = (f32[2,4,8,8,128]{4,3,2,1,0:T(8,128)S(1)}, f32[32]{0:T(128)S(1)}) custom-call(f32[2,4,8,8,128]{4,3,2,1,0:T(8,128)} %adj.1, f32[4,4,8,8,128]{4,3,2,1,0:T(8,128)} %saved.1, f32[3,8,8,128]{3,2,1,0:T(8,128)} %wind.1, s32[8,8,128]{2,1,0:T(8,128)} %slot.1, s32[1,1,1,64]{3,2,1,0:T(1,128)} %table.1, f32[128,128]{1,0:T(8,128)} %bitcast.1), custom_call_target="tpu_custom_call" | custom-call | tf_op jit(solution)/shard_map/pallas_call | solution.py:471
  23.2 0.7 %copy.10 = f32[2,4,8,8,128]{4,3,2,1,0:T(8,128)} copy(f32[2,4,8,8,128]{4,3,2,1,0:T(8,128)S(1)} %get-tuple-element.4) | data formatting | bytes 524288
  23.9 0.5 %copy.11 = f32[32]{0:T(128)} copy(f32[32]{0:T(128)S(1)} %get-tuple-element.5) | data formatting | bytes 256

commit v5 on v4

--- a/solution.py
+++ b/solution.py
@@ -45,7 +45,7 @@
 def kernel(sizes, adj, saved, wind, slot, table, impedance, out, grad,
            mid, upp, sav, win, slo, tab, imp, ext, part, prod,
            xbuf, xzbuf, ybuf, xybuf, zbuf, xr, xzr, yr, yzr, zr, xyr, xyzr,
-           xs, ys, zs, xf, yf, zf, smat, gs, gr,
+           xs, ys, zs, xf, yf, zf, slots, smat, gs, gr,
            in_sem, ss, rs, fs, fr, g_ss, g_rs):
     nx, ny, nz = sizes
     ix, iy, iz = lax.axis_index("gx"), lax.axis_index("gy"), lax.axis_index("gz")
@@ -200,22 +200,25 @@
         xybuf[0, side] = xy_high
         xybuf[1, side] = xy_low
 
-    halo = []
-
-    def post(src, dst, to, dx=0):
-        i = len(halo)
+    halo = {}
+
+    def post(kind, src, dst, to, dx=0):
+        i = sum(len(group) for group in halo.values())
         send_if, recv_if = {0: (None, None), 1: (has_right, has_left), -1: (has_left, has_right)}[dx]
-        halo.append(Sent(src, dst, ss.at[i], rs.at[i], to, send_if, recv_if))
-
-    post(zbuf, zr, device(0, 0, 1))
-    for side, d in ((0, 1), (1, -1)):
-        post(xbuf.at[side], xr.at[side], device(d, 0, 0), d)
-        post(xzbuf.at[side], xzr.at[side], device(d, 0, 1), d)
-        post(ybuf.at[side], yr.at[side], device(0, d, 0))
-        post(ybuf.at[side, 0], yzr.at[side], device(0, d, 1))
-        for x_side, e in ((0, 1), (1, -1)):
-            post(xybuf.at[x_side, side], xyr.at[x_side, side], device(e, d, 0), e)
-            post(xybuf.at[x_side, side], xyzr.at[x_side, side], device(e, d, 1), e)
+        halo.setdefault(kind, []).append(Sent(src, dst, ss.at[i], rs.at[i], to, send_if, recv_if))
+
+    both = ((0, 1), (1, -1))
+    post("z", zbuf, zr, device(0, 0, 1))
+    for side, d in both:
+        post("xz", xzbuf.at[side], xzr.at[side], device(d, 0, 1), d)
+        post("yz", ybuf.at[side, 0], yzr.at[side], device(0, d, 1))
+        for x_side, e in both:
+            post("xyz", xybuf.at[x_side, side], xyzr.at[x_side, side], device(e, d, 1), e)
+    for side, d in both:
+        for x_side, e in both:
+            post("xy", xybuf.at[x_side, side], xyr.at[x_side, side], device(e, d, 0), e)
+        post("y", ybuf.at[side], yr.at[side], device(0, d, 0))
+        post("x", xbuf.at[side], xr.at[side], device(d, 0, 0), d)
 
     @pl.when(has_left & has_right)
     def _():
@@ -231,11 +234,17 @@
         pl.semaphore_wait(barrier, 12)
         pl.semaphore_signal(barrier, inc=1, device_id=(0, iy, iz), device_id_type=MESH)
 
-    for sent in halo:
-        sent.start()
-
-    def add_products(k, base):
-        for z in range(8):
+    for group in halo.values():
+        for sent in group:
+            sent.start()
+
+    def arrived(*kinds):
+        for kind in kinds:
+            for sent in halo[kind]:
+                sent.wait_recv()
+
+    def add_products(k, base, planes):
+        for z in planes:
             zi = plane(z)
             total = get(base, z, OWN) * sav[k, 0, zi]
             for c in range(1, 4):
@@ -243,9 +252,7 @@
             prod[z] = total if k == 0 else prod[z] + total
 
     loads[6].wait()
-    add_products(0, 0)
-    for sent in halo:
-        sent.wait_recv()
+    add_products(0, 0, range(8))
 
     def masked(f, t, value):
         if f < 4 or WIND <= f < DAMP:
@@ -255,39 +262,43 @@
     def both_y(high, low):
         return jnp.where(quarter < 2, high, low)
 
-    y_own = [both_y(yr[0, t], yr[1, t]) for t in range(3)]
-    y_top = both_y(yzr[0], yzr[1])
-
     def xy_tile(src, t):
         value = jnp.where(row // 2 == t, both_y(src[0, 0], src[0, 1]), both_y(src[1, 0], src[1, 1]))
         return pltpu.roll(value, (6 - 2 * t) % 8, 0)
 
-    xy_own = [xy_tile(xyr, t) for t in range(3)]
-    xy_top = xy_tile(xyzr, 0)
-    for z in range(8):
+    def each(run):
+        for z in range(8):
+            for f in range(FIELDS):
+                run(z, f, (7 - z) * FIELDS + f)
+
+    def unpack_x(z, f, n):
+        k = n % 4
+        value = jnp.where(row // 2 == k, xr[0, n // 4], xr[1, n // 4])
+        put(f, z, XH, masked(f, XH, pltpu.roll(value, (6 - 2 * k) % 8, 0)))
+
+    def unpack_y(z, f, n):
+        put(f, z, YH, masked(f, YH, pltpu.roll(y_own[n // 32], (126 - 4 * (n % 32)) % 128, 1)))
+
+    def unpack_xy(z, f, n):
+        if f < DAMP:
+            put(f, z, XYH, masked(f, XYH, pltpu.roll(xy_own[n // 32], (126 - 4 * (n % 32)) % 128, 1)))
+
+    def unpack_top():
+        y_top = both_y(yzr[0], yzr[1])
+        xy_top = xy_tile(xyzr, 0)
         for f in range(FIELDS):
-            n = (7 - z) * FIELDS + f
-            k = n % 4
-            value = jnp.where(row // 2 == k, xr[0, n // 4], xr[1, n // 4])
-            put(f, z, XH, masked(f, XH, pltpu.roll(value, (6 - 2 * k) % 8, 0)))
-            t, k = n // 32, n % 32
-            shift = (126 - 4 * k) % 128
-            put(f, z, YH, masked(f, YH, pltpu.roll(y_own[t], shift, 1)))
+            put(f, 8, OWN, zr[f])
+            if 4 <= f <= WIND:
+                put(f, 9, OWN, zr[FIELDS + f - 4])
+            if f < WIND + 2:
+                value = jnp.where(row == 7, xzr[0, pl.ds(f, 1), :], xzr[1, pl.ds(f, 1), :])
+                put(f, 8, XH, masked(f, XH, value))
+            shift = (126 - 4 * f) % 128
             if f < DAMP:
-                put(f, z, XYH, masked(f, XYH, pltpu.roll(xy_own[t], shift, 1)))
-    for f in range(FIELDS):
-        put(f, 8, OWN, zr[f])
-        if 4 <= f <= WIND:
-            put(f, 9, OWN, zr[FIELDS + f - 4])
-        if f < WIND + 2:
-            value = jnp.where(row == 7, xzr[0, pl.ds(f, 1), :], xzr[1, pl.ds(f, 1), :])
-            put(f, 8, XH, masked(f, XH, value))
-        shift = (126 - 4 * f) % 128
-        if f < DAMP:
-            put(f, 8, YH, masked(f, YH, pltpu.roll(y_top, shift, 1)))
-        if f < 4 or WIND <= f < DAMP:
-            put(f, 8, XYH, masked(f, XYH, pltpu.roll(xy_top, shift, 1)))
-            put(f, 9, YH, masked(f, YH, pltpu.roll(y_top, (126 - 4 * (FIELDS + f)) % 128, 1)))
+                put(f, 8, YH, masked(f, YH, pltpu.roll(y_top, shift, 1)))
+            if f < 4 or WIND <= f < DAMP:
+                put(f, 8, XYH, masked(f, XYH, pltpu.roll(xy_top, shift, 1)))
+                put(f, 9, YH, masked(f, YH, pltpu.roll(y_top, (126 - 4 * (FIELDS + f)) % 128, 1)))
 
     def across(own, far, r_up, r_dn, axis):
         size = own.shape[axis]
@@ -309,46 +320,54 @@
         size = flux.shape[axis]
         return jnp.where(r_up, pltpu.roll(flux, size - 1, axis), 0.0) - jnp.where(r_dn, pltpu.roll(flux, 1, axis), 0.0)
 
-    def first_step():
-        beside_x = {OWN: XH, XH: OWN, YH: XYH, XYH: YH}
-        beside_y = {OWN: YH, YH: OWN, XH: XYH, XYH: XH}
-        here = None
-        after = flux_plane(0, 0, [OWN, XH, YH, XYH])
-        for z in range(10):
-            before, here = here, after
-            after = None
-            if z + 1 < 9:
-                after = flux_plane(0, z + 1, [OWN, XH, YH, XYH])
-                if z + 1 == 8:
-                    fz = after[XH][0]
-                    for c in range(4):
-                        lo, hi = xzr[0, pl.ds(10 + c, 1), :], xzr[1, pl.ds(10 + c, 1), :]
-                        fz[c] = jnp.where(row == 6, lo, jnp.where(row == 1, hi, fz[c]))
-            elif z + 1 == 9:
-                fx = []
-                for c in range(4):
-                    lo, hi = xzr[0, pl.ds(14 + c, 1), :], xzr[1, pl.ds(14 + c, 1), :]
-                    fx.append(jnp.where(inside[XH], jnp.where(row == 7, lo, hi), 0.0))
-                after = {XH: (None, fx, None), YH: flux_tile(0, 9, YH)}
-            for t in [OWN, XH, YH, XYH] if z < 8 else [OWN, XH, YH] if z == 8 else [OWN]:
+    every, sides = [OWN, XH, YH, XYH], [OWN, XH, YH]
+    beside_x = {OWN: XH, XH: OWN, YH: XYH, XYH: YH}
+    beside_y = {OWN: YH, YH: OWN, XH: XYH, XYH: XH}
+
+    def first_plane(z):
+        if z < 8:
+            return flux_plane(0, z, every)
+        if z == 8:
+            result = flux_plane(0, 8, every)
+            fz = result[XH][0]
+            for c in range(4):
+                lo, hi = xzr[0, pl.ds(10 + c, 1), :], xzr[1, pl.ds(10 + c, 1), :]
+                fz[c] = jnp.where(row == 6, lo, jnp.where(row == 1, hi, fz[c]))
+            return result
+        fx = []
+        for c in range(4):
+            lo, hi = xzr[0, pl.ds(14 + c, 1), :], xzr[1, pl.ds(14 + c, 1), :]
+            fx.append(jnp.where(inside[XH], jnp.where(row == 7, lo, hi), 0.0))
+        return {XH: (None, fx, None), YH: flux_tile(0, 9, YH)}
+
+    def first_step(planes):
+        held = {}
+        for z in planes:
+            for w in ([z - 1, z] if z == 8 else [z, z + 1] if z == 7 else [z]):
+                if w not in held:
+                    held[w] = first_plane(w)
+            here = held[z]
+            for t in every if z < 8 else sides if z == 8 else [OWN]:
                 for c in range(4):
                     sx = seam(here[beside_x[t]][1][c], row7, row0, 0)
                     sy = seam(here[beside_y[t]][2][c], lane127, lane0, 1)
                     value = get(4 + c, z, t) + HALF * (sx + sy)
                     if z == 7:
-                        value = value + hz * after[t][0][c]
+                        value = value + hz * held[8][t][0][c]
                     if z == 8:
-                        value = value - hz * before[t][0][c]
+                        value = value - hz * held[7][t][0][c]
                     if t != OWN:
                         value = jnp.where(inside[t], value, 0.0)
                     put(4 + c, z, t, value)
 
-    def step(src, dst, flux_tiles, new_tiles, keep=None):
-        before, here = None, flux_plane(src, 0, flux_tiles[0])
-        for z in range(len(new_tiles)):
-            after = flux_plane(src, z + 1, flux_tiles[z + 1])
+    def step(src, dst, planes, flux_tiles, new_tiles, keep=None):
+        held = {}
+        for z in planes:
+            for w in (z - 1, z, z + 1):
+                if w >= 0 and w not in held:
+                    held[w] = flux_plane(src, w, flux_tiles[w])
+            f = held[z]
             for c in range(4):
-                f = {t: here[t] for t in flux_tiles[z]}
                 dx, dy = {}, {}
                 dx[OWN], dx[XH] = across(f[OWN][1][c], f[XH][1][c], row7, row0, 0)
                 dy[OWN], dy[YH] = across(f[OWN][2][c], f[YH][2][c], lane127, lane0, 1)
@@ -356,34 +375,81 @@
                     dx[YH], dx[XYH] = across(f[YH][1][c], f[XYH][1][c], row7, row0, 0)
                     dy[XH], dy[XYH] = across(f[XH][2][c], f[XYH][2][c], lane127, lane0, 1)
                 for t in new_tiles[z]:
-                    up = after[t][0][c]
-                    dz = up if before is None else up - before[t][0][c]
+                    dz = held[z + 1][t][0][c]
+                    if z > 0:
+                        dz = dz - held[z - 1][t][0][c]
                     value = get(dst + c, z, t) + HALF * (dx[t] + dy[t]) + hz * dz - get(DAMP, z, t) * get(src + c, z, t)
                     if t != OWN:
                         value = jnp.where(inside[t], value, 0.0)
                     put(dst + c, z, t, value)
                     if keep is not None:
                         keep(c, z, value)
-            before, here = here, after
-
-    every = [OWN, XH, YH, XYH]
-    sides = [OWN, XH, YH]
-    first_step()
-    add_products(1, 4)
-    step(4, 0, [every] * 8 + [sides, [OWN]], [sides] * 8 + [[OWN]])
-    add_products(2, 0)
-    third = [[None] * 8 for _ in range(4)]
+
+    def second_step(planes):
+        step(4, 0, planes, [every] * 8 + [sides, [OWN]], [sides] * 8 + [[OWN]])
 
     def keep(c, z, value):
-        third[c][z] = value
         out[0, c, plane(z)] = value
 
-    step(0, 4, [sides] * 8 + [[OWN]], [[OWN]] * 8, keep)
+    def third_step(planes):
+        step(0, 4, planes, [sides] * 8 + [[OWN]], [[OWN]] * 8, keep)
+
+    arrived("x")
+    each(unpack_x)
+    arrived("y")
+    y_own = [both_y(yr[0, t], yr[1, t]) for t in range(3)]
+    each(unpack_y)
+    arrived("xy")
+    xy_own = [xy_tile(xyr, t) for t in range(3)]
+    each(unpack_xy)
+    first_step(range(7))
+    add_products(1, 4, range(7))
+    second_step(range(6))
+    add_products(2, 0, range(6))
+    third_step(range(5))
+    add_products(3, 4, range(5))
+
+    def slot_sum(s, planes):
+        total = zero
+        for z in planes:
+            total = total + jnp.where(slo[plane(z)] == s + 1, prod[z], 0.0)
+        return total
+
+    for s in range(64):
+        slots[s] = slot_sum(s, range(5))
+    turned = jnp.transpose(jnp.broadcast_to(place[0:1], (128, 128)))[0:64]
+    wide = lax.broadcasted_iota(jnp.int32, (64, 128), 1)
+    arrived("z", "yz", "xz", "xyz")
+    unpack_top()
+    first_step(range(7, 10))
+    add_products(1, 4, [7])
+    second_step(range(6, 9))
+    add_products(2, 0, [6, 7])
+    third_step(range(5, 8))
+    add_products(3, 4, [5, 6, 7])
+
+    for s in range(64):
+        total = slots[s] + slot_sum(s, range(5, 8))
+        smat[pl.ds(s, 1), :] = jnp.sum(total, axis=0, keepdims=True)
+    sums = jnp.sum(smat[...], axis=1, keepdims=True) * (-FULL)
+    facades = jnp.sum(jnp.where(turned == wide, sums, 0.0), axis=0, keepdims=True)
+    gs[...] = jnp.broadcast_to(facades, (8, 128))
+
+    @pl.when(ix == 0)
+    def _():
+        pl.semaphore_wait(barrier, 1)
+
+    parts = [
+        Sent(gs, gr.at[0], g_ss.at[0], g_rs.at[0], device(1, 0, 0)),
+        Sent(gs, gr.at[1], g_ss.at[1], g_rs.at[1], device(-1, 0, 0)),
+    ]
+    for sent in parts:
+        sent.start()
 
     low, high = zero, zero
     allf = []
     for z in range(8):
-        fz, fx, fy = fluxes([third[c][z] for c in range(4)], [get(WIND + c, z, OWN) for c in range(3)])
+        fz, fx, fy = fluxes([get(4 + c, z, OWN) for c in range(4)], [get(WIND + c, z, OWN) for c in range(3)])
         allf.append((fz, fx, fy))
         for c in range(4):
             n = c * 8 + z
@@ -405,34 +471,10 @@
     ]
     for sent in faces:
         sent.start()
-    add_products(3, 4)
-
-    for s in range(64):
-        total = zero
-        for z in range(8):
-            total = total + jnp.where(slo[plane(z)] == s + 1, prod[z], 0.0)
-        smat[pl.ds(s, 1), :] = jnp.sum(total, axis=0, keepdims=True)
-    sums = jnp.sum(smat[...], axis=1, keepdims=True) * (-FULL)
-    turned = jnp.transpose(jnp.broadcast_to(place[0:1], (128, 128)))[0:64]
-    wide = lax.broadcasted_iota(jnp.int32, (64, 128), 1)
-    facades = jnp.sum(jnp.where(turned == wide, sums, 0.0), axis=0, keepdims=True)
-    gs[...] = jnp.broadcast_to(facades, (8, 128))
-
-    @pl.when(ix == 0)
-    def _():
-        pl.semaphore_wait(barrier, 1)
-
-    parts = [
-        Sent(gs, gr.at[0], g_ss.at[0], g_rs.at[0], device(1, 0, 0)),
-        Sent(gs, gr.at[1], g_ss.at[1], g_rs.at[1], device(-1, 0, 0)),
-    ]
-    for sent in parts:
-        sent.start()
-
     def hold(c, z, value):
         part[c * 8 + z] = value
 
-    within(lambda c, z: third[c][z], allf, lambda c, z: get(c, z, OWN), hold)
+    within(lambda c, z: get(4 + c, z, OWN), allf, lambda c, z: get(c, z, OWN), hold)
 
     for sent in faces:
         sent.wait_recv()
@@ -456,8 +498,18 @@
         sent.wait_recv()
     total = gs[...] + pltpu.roll(gr[0], 96, 1) + pltpu.roll(gr[1], 64, 1)
     grad[...] = total[0, 0:FAC_DEV]
-    for sent in halo + faces + parts:
+    for sent in sum(halo.values(), []) + faces + parts:
         sent.wait_send()
+
+
+def writer(state, sums, out, grad, sems):
+    copies = [pltpu.make_async_copy(sums, grad, sems.at[0])]
+    for level in range(2):
+        copies.append(pltpu.make_async_copy(state.at[level], out.at[level], sems.at[1 + level]))
+    for copy in copies:
+        copy.start()
+    for copy in copies:
+        copy.wait()
 
 
 def local(sizes, adjoint, saved_state, wind_field, facade_slot, facade_table, impedance):
@@ -468,7 +520,7 @@
     dma = pltpu.SemaphoreType.DMA
     steps = saved_state.shape[0]
     assert steps == 4
-    out, grad = pl.pallas_call(
+    state, sums = pl.pallas_call(
         functools.partial(kernel, sizes),
         out_shape=[
             jax.ShapeDtypeStruct(adjoint.shape, F32),
@@ -505,6 +557,7 @@
             v((2, 32, 128), F32),
             v((2, 8, 128), F32),
             v((4, 8, 128), F32),
+            v((64, 8, 128), F32),
             v((64, 128), F32),
             v((8, 128), F32),
             v((2, 8, 128), F32),
@@ -515,6 +568,17 @@
         ),
     )(*[pltpu.with_memory_space_constraint(a, pltpu.HBM)
         for a in (adjoint, saved_state, wind_field, facade_slot, facade_table, imp)])
+    out, grad = pl.pallas_call(
+        writer,
+        out_shape=[
+            jax.ShapeDtypeStruct(adjoint.shape, F32),
+            jax.ShapeDtypeStruct((FAC_DEV,), F32),
+        ],
+        in_specs=[vmem_spec, vmem_spec],
+        out_specs=[hbm_spec, hbm_spec],
+        scratch_shapes=[dma((3,))],
+        compiler_params=pltpu.CompilerParams(vmem_limit_bytes=1 << 20),
+    )(state, sums)
     return out, grad
 
 

time: 24.6 us -> 23.6 us (0.959)
  local copies, waits for them, and re-layouts: 1.22 us -> 0 us
    unnamed x2 -> x0, local copies, waits for them, and re-layouts: 1.22 us -> none
    pallas_call x0 -> x1, Pallas kernels: none -> 0.73 us  [local(): pl.pallas_call(writer, out_shape=[jax.ShapeDtypeStruct(adjoint.shape, F32...]
    pallas_call x1, Pallas kernels: 22.6 us -> 22.1 us  [local(): pl.pallas_call(functools.partial(kernel, sizes), out_shape=[jax.ShapeDtyp...]
where the time goes in v5:
time: 23.6 us; the launch traced here: 23.5 us
  Pallas kernels  22.8 us (97%)
  between operations  0.64 us (3%)
    pallas_call x1, Pallas kernels, local(): pl.pallas_call(functools.partial(kernel, sizes), out_shape=[jax.ShapeDtyp...  22.1 us
    pallas_call x1, Pallas kernels, local(): pl.pallas_call(writer, out_shape=[jax.ShapeDtypeStruct(adjoint.shape, F32...  0.73 us

profile of v5, /device:TPU:2, one launch (start us, length us, event | category | flops | bytes accessed | tf_op | source)
XLA Modules:
  0.0 23.5 jit_solution(4043056066471942069)
XLA Ops:
  0.6 22.1 %shard_map.77 = (f32[2,4,8,8,128]{4,3,2,1,0:T(8,128)S(1)}, f32[32]{0:T(128)S(1)}) custom-call(f32[2,4,8,8,128]{4,3,2,1,0:T(8,128)} %adj.1, f32[4,4,8,8,128]{4,3,2,1,0:T(8,128)} %saved.1, f32[3,8,8,128]{3,2,1,0:T(8,128)} %wind.1, s32[8,8,128]{2,1,0:T(8,128)} %slot.1, s32[1,1,1,64]{3,2,1,0:T(1,128)} %table.1, f32[128,128]{1,0:T(8,128)} %bitcast.1), custom_call_target="tpu_custom_call" | custom-call | tf_op jit(solution)/shard_map/pallas_call | solution.py:523
  22.7 0.7 %shard_map.78 = (f32[2,4,8,8,128]{4,3,2,1,0:T(8,128)}, f32[32]{0:T(128)}) custom-call(f32[2,4,8,8,128]{4,3,2,1,0:T(8,128)S(1)} %get-tuple-element.4.state, f32[32]{0:T(128)S(1)} %get-tuple-element.5.sums), custom_call_target="tpu_custom_call" | custom-call | tf_op jit(solution)/shard_map/pallas_call | solution.py:571

commit v6 on v5

--- a/solution.py
+++ b/solution.py
@@ -208,17 +208,17 @@
         halo.setdefault(kind, []).append(Sent(src, dst, ss.at[i], rs.at[i], to, send_if, recv_if))
 
     both = ((0, 1), (1, -1))
+    for side, d in both:
+        for x_side, e in both:
+            post("xy", xybuf.at[x_side, side], xyr.at[x_side, side], device(e, d, 0), e)
+        post("y", ybuf.at[side], yr.at[side], device(0, d, 0))
+        post("x", xbuf.at[side], xr.at[side], device(d, 0, 0), d)
     post("z", zbuf, zr, device(0, 0, 1))
     for side, d in both:
         post("xz", xzbuf.at[side], xzr.at[side], device(d, 0, 1), d)
         post("yz", ybuf.at[side, 0], yzr.at[side], device(0, d, 1))
         for x_side, e in both:
             post("xyz", xybuf.at[x_side, side], xyzr.at[x_side, side], device(e, d, 1), e)
-    for side, d in both:
-        for x_side, e in both:
-            post("xy", xybuf.at[x_side, side], xyr.at[x_side, side], device(e, d, 0), e)
-        post("y", ybuf.at[side], yr.at[side], device(0, d, 0))
-        post("x", xbuf.at[side], xr.at[side], device(d, 0, 0), d)
 
     @pl.when(has_left & has_right)
     def _():
@@ -234,9 +234,14 @@
         pl.semaphore_wait(barrier, 12)
         pl.semaphore_signal(barrier, inc=1, device_id=(0, iy, iz), device_id_type=MESH)
 
-    for group in halo.values():
+    early = lax.rem(ix, 2) == 1
+    for kind, group in halo.items():
         for sent in group:
-            sent.start()
+            if kind == "z":
+                pl.when(early)(sent.start)
+            else:
+                sent.start()
+    pl.when(jnp.logical_not(early))(halo["z"][0].start)
 
     def arrived(*kinds):
         for kind in kinds:

time: 23.6 us -> 22.4 us (0.949)
  the two profiles are of different devices: /device:TPU:2 before, /device:TPU:4 now
where the time goes in v6:
time: 22.4 us; the launch traced here: 22.3 us
  Pallas kernels  21.7 us (97%)
  between operations  0.64 us (3%)
    pallas_call x1, Pallas kernels, local(): pl.pallas_call(functools.partial(kernel, sizes), out_shape=[jax.ShapeDtyp...  20.9 us
    pallas_call x1, Pallas kernels, local(): pl.pallas_call(writer, out_shape=[jax.ShapeDtypeStruct(adjoint.shape, F32...  0.73 us

profile of v6, /device:TPU:4, one launch (start us, length us, event | category | flops | bytes accessed | tf_op | source)
XLA Modules:
  0.0 22.3 jit_solution(8960178793984030633)
XLA Ops:
  0.6 20.9 %shard_map.77 = (f32[2,4,8,8,128]{4,3,2,1,0:T(8,128)S(1)}, f32[32]{0:T(128)S(1)}) custom-call(f32[2,4,8,8,128]{4,3,2,1,0:T(8,128)} %adj.1, f32[4,4,8,8,128]{4,3,2,1,0:T(8,128)} %saved.1, f32[3,8,8,128]{3,2,1,0:T(8,128)} %wind.1, s32[8,8,128]{2,1,0:T(8,128)} %slot.1, s32[1,1,1,64]{3,2,1,0:T(1,128)} %table.1, f32[128,128]{1,0:T(8,128)} %bitcast.1), custom_call_target="tpu_custom_call" | custom-call | tf_op jit(solution)/shard_map/pallas_call | solution.py:528
  21.6 0.7 %shard_map.78 = (f32[2,4,8,8,128]{4,3,2,1,0:T(8,128)}, f32[32]{0:T(128)}) custom-call(f32[2,4,8,8,128]{4,3,2,1,0:T(8,128)S(1)} %get-tuple-element.4.state, f32[32]{0:T(128)S(1)} %get-tuple-element.5.sums), custom_call_target="tpu_custom_call" | custom-call | tf_op jit(solution)/shard_map/pallas_call | solution.py:576

commit v7 on v6

--- a/solution.py
+++ b/solution.py
@@ -234,14 +234,15 @@
         pl.semaphore_wait(barrier, 12)
         pl.semaphore_signal(barrier, inc=1, device_id=(0, iy, iz), device_id_type=MESH)
 
-    early = lax.rem(ix, 2) == 1
-    for kind, group in halo.items():
-        for sent in group:
-            if kind == "z":
-                pl.when(early)(sent.start)
-            else:
+    odd = lax.rem(ix, 2) == 1
+
+    def start(*kinds):
+        for kind in kinds:
+            for sent in halo[kind]:
                 sent.start()
-    pl.when(jnp.logical_not(early))(halo["z"][0].start)
+
+    pl.when(odd)(lambda: start("y", "yz", "z", "x", "xy", "xz", "xyz"))
+    pl.when(jnp.logical_not(odd))(lambda: start("x", "xy", "xz", "xyz", "y", "yz", "z"))
 
     def arrived(*kinds):
         for kind in kinds:

time: 22.4 us -> 22.2 us (level)
  Pallas kernels: 21.7 us -> 21.4 us
    pallas_call x1, Pallas kernels: 20.9 us -> 20.7 us  [local(): pl.pallas_call(functools.partial(kernel, sizes), out_shape=[jax.ShapeDtyp...]
where the time goes in v7:
time: 22.2 us; the launch traced here: 22 us
  Pallas kernels  21.4 us (96%)
  between operations  0.64 us (3%)
    pallas_call x1, Pallas kernels, local(): pl.pallas_call(functools.partial(kernel, sizes), out_shape=[jax.ShapeDtyp...  20.7 us
    pallas_call x1, Pallas kernels, local(): pl.pallas_call(writer, out_shape=[jax.ShapeDtypeStruct(adjoint.shape, F32...  0.73 us

profile of v7, /device:TPU:4, one launch (start us, length us, event | category | flops | bytes accessed | tf_op | source)
XLA Modules:
  0.0 22.0 jit_solution(2373656714443955248)
XLA Ops:
  0.6 20.7 %shard_map.77 = (f32[2,4,8,8,128]{4,3,2,1,0:T(8,128)S(1)}, f32[32]{0:T(128)S(1)}) custom-call(f32[2,4,8,8,128]{4,3,2,1,0:T(8,128)} %adj.1, f32[4,4,8,8,128]{4,3,2,1,0:T(8,128)} %saved.1, f32[3,8,8,128]{3,2,1,0:T(8,128)} %wind.1, s32[8,8,128]{2,1,0:T(8,128)} %slot.1, s32[1,1,1,64]{3,2,1,0:T(1,128)} %table.1, f32[128,128]{1,0:T(8,128)} %bitcast.1), custom_call_target="tpu_custom_call" | custom-call | tf_op jit(solution)/shard_map/pallas_call | solution.py:529
  21.3 0.7 %shard_map.78 = (f32[2,4,8,8,128]{4,3,2,1,0:T(8,128)}, f32[32]{0:T(128)}) custom-call(f32[2,4,8,8,128]{4,3,2,1,0:T(8,128)S(1)} %get-tuple-element.4.state, f32[32]{0:T(128)S(1)} %get-tuple-element.5.sums), custom_call_target="tpu_custom_call" | custom-call | tf_op jit(solution)/shard_map/pallas_call | solution.py:577

commit v8 on v7

--- a/solution.py
+++ b/solution.py
@@ -500,12 +500,12 @@
             if z == 7:
                 value = value + hz * zf[c]
             out[1, c, plane(z)] = value
+    for sent in sum(halo.values(), []) + faces + parts:
+        sent.wait_send()
     for sent in parts:
         sent.wait_recv()
     total = gs[...] + pltpu.roll(gr[0], 96, 1) + pltpu.roll(gr[1], 64, 1)
     grad[...] = total[0, 0:FAC_DEV]
-    for sent in sum(halo.values(), []) + faces + parts:
-        sent.wait_send()
 
 
 def writer(state, sums, out, grad, sems):

time: 22.2 us -> 22.2 us (level)
  no operation moved by 1% of the time
where the time goes in v8:
time: 22.2 us; the launch traced here: 22 us
  Pallas kernels  21.4 us (96%)
  between operations  0.64 us (3%)
    pallas_call x1, Pallas kernels, local(): pl.pallas_call(functools.partial(kernel, sizes), out_shape=[jax.ShapeDtyp...  20.6 us
    pallas_call x1, Pallas kernels, local(): pl.pallas_call(writer, out_shape=[jax.ShapeDtypeStruct(adjoint.shape, F32...  0.73 us

profile of v8, /device:TPU:4, one launch (start us, length us, event | category | flops | bytes accessed | tf_op | source)
XLA Modules:
  0.0 22.0 jit_solution(16064625320852668272)
XLA Ops:
  0.6 20.6 %shard_map.77 = (f32[2,4,8,8,128]{4,3,2,1,0:T(8,128)S(1)}, f32[32]{0:T(128)S(1)}) custom-call(f32[2,4,8,8,128]{4,3,2,1,0:T(8,128)} %adj.1, f32[4,4,8,8,128]{4,3,2,1,0:T(8,128)} %saved.1, f32[3,8,8,128]{3,2,1,0:T(8,128)} %wind.1, s32[8,8,128]{2,1,0:T(8,128)} %slot.1, s32[1,1,1,64]{3,2,1,0:T(1,128)} %table.1, f32[128,128]{1,0:T(8,128)} %bitcast.1), custom_call_target="tpu_custom_call" | custom-call | tf_op jit(solution)/shard_map/pallas_call | solution.py:529
  21.3 0.7 %shard_map.78 = (f32[2,4,8,8,128]{4,3,2,1,0:T(8,128)}, f32[32]{0:T(128)}) custom-call(f32[2,4,8,8,128]{4,3,2,1,0:T(8,128)S(1)} %get-tuple-element.4.state, f32[32]{0:T(128)S(1)} %get-tuple-element.5.sums), custom_call_target="tpu_custom_call" | custom-call | tf_op jit(solution)/shard_map/pallas_call | solution.py:577
